TPU v7x, 32 devices: a whole 2x2x4 slice. The times are simulated.
32 devices in a mesh: row: 16 (over z, y, core), col: 2 (over x).
Axes of the slice: x: 2, y: 2, z: 4, core: 2. Of those that a mesh axis runs over, the one named last changes fastest.
Arguments:
- weight: float32 [25600, 5120], P('row', 'col'), may hold values from -6 to 6
- grad: float32 [25600, 5120], P('row', 'col'), may hold values from -6 to 6
- momentum: float32 [25600, 5120], P('row', 'col'), may hold values from -90 to 90
- right_factor: bfloat16 [5120, 256], P('col'), may hold values from -0.078125 to 0.078125
Outputs:
- new_weight: float32 [25600, 5120], P('row', 'col')
- new_momentum: float32 [25600, 5120], P('row', 'col')
- new_right: bfloat16 [5120, 256], P(('col', 'row'))
All inputs are finite; a program needn't handle non-finite values.
Results may differ from a plain program's by a relative error of at most 0.0023.
Values sent between devices are 32-bit elements; how exact they have to be, the bound alone decides.
No kernel may reach another device: no remote copies, remote signals or barrier semaphores. Data moves between devices by JAX's collectives and lax.ppermute only.
A program may use at most 128 MiB of HBM per device.

v0:
```python
import functools
import math

import jax
import jax.numpy as jnp
from jax import lax
from jax.experimental import pallas as pl
from jax.experimental.pallas import tpu as pltpu
from jax.sharding import PartitionSpec as P

feedback_share = 0.05
decay_keep = 0.999
step_rate = 0.5
epsilon = 1e-06
highest = lax.Precision.HIGHEST
MIB = 1 << 20
VMEM = pl.BlockSpec(memory_space=pltpu.VMEM)
SMEM = pl.BlockSpec(memory_space=pltpu.SMEM)
ANY = pl.BlockSpec(memory_space=pl.ANY)


def in_hbm(x):
    return pltpu.with_memory_space_constraint(x, pltpu.HBM)


def cost(microseconds):
    return pl.CostEstimate(flops=int(microseconds * 1153e6), bytes_accessed=0, transcendentals=0)


def largest_divisor(total, limit, multiple):
    for size in range(min(limit, total), 0, -1):
        if total % size == 0 and size % multiple == 0:
            return size
    return total


def split(x):
    high = x.astype(jnp.bfloat16)
    low = (x - high.astype(jnp.float32)).astype(jnp.bfloat16)
    return high, low


def mul(a, b, dims=(((1,), (0,)), ((), ()))):
    return lax.dot_general(a, b, dims, preferred_element_type=jnp.float32)


TRANSPOSED = (((0,), (0,)), ((), ()))
BOTH_LAST = (((1,), (1,)), ((), ()))


def partial_kernel(start, counts, tile, momentum, grad, right_factor, *refs):
    count = len(counts)
    high_out, low_out, *partials = refs[-2 - count :]

    def step(m, g, h, l, out):
        high, low = split(m[...] + g[...])
        h[...] = high
        l[...] = low
        both = mul(jnp.concatenate([high, low], axis=0), right_factor[...])
        out[...] = both[:tile] + both[tile:]

    columns = momentum.shape[1]
    wide = pl.BlockSpec((tile, columns), lambda i: (i, 0))
    thin = pl.BlockSpec((tile, right_factor.shape[1]), lambda i: (i, 0))
    for rows, partial in zip(counts, partials):
        at = pl.ds(start, rows)
        pltpu.emit_pipeline(step, grid=(rows // tile,), in_specs=[wide, wide], out_specs=[wide, wide, thin])(
            momentum.at[at], grad.at[at], high_out.at[at], low_out.at[at], partial
        )
        start += rows


def partial_products(start, counts, momentum, grad, right_factor, halves, *earlier):
    columns, rank = right_factor.shape
    tile = largest_divisor(math.gcd(*counts), 192, 64)
    halves = [] if halves is None else [in_hbm(x) for x in halves]
    shapes = [pltpu.HBM(momentum.shape, jnp.bfloat16)] * 2
    shapes += [pltpu.HBM((rows, rank), jnp.float32) for rows in counts]
    out = pl.pallas_call(
        functools.partial(partial_kernel, start, counts, tile),
        out_shape=shapes,
        in_specs=[ANY, ANY, VMEM] + [ANY] * (len(halves) + len(earlier)),
        out_specs=[ANY] * len(shapes),
        input_output_aliases={3 + i: i for i in range(len(halves))},
        compiler_params=pltpu.CompilerParams(vmem_limit_bytes=16 * MIB),
        cost_estimate=cost(sum(counts) / 100),
        name="partial_proj",
    )(in_hbm(momentum), in_hbm(grad), right_factor, *halves, *earlier)
    return out[:2], out[2:]


def project_kernel(start, widths, step, first, pieces, place, high_in, low_in, before, *refs):
    count = len(widths)
    mine, theirs, refs = refs[:pieces], refs[pieces : 2 * pieces], refs[2 * pieces :]
    sums_in = None if first else refs[:count]
    proj, *sums, turned = refs[0 if first else count :]
    base = 0
    for m, t in zip(mine, theirs):
        proj[base : base + m.shape[0], :] = m[...] + t[...]
        base += m.shape[0]
    value = proj[...]
    rows, rank = value.shape
    block = rank // 8
    turned[...] = value.T
    ordered = jnp.concatenate(
        [turned[pl.ds(pl.multiple_of((place[0] ^ r) * block, block), block), :] for r in range(8)], axis=0
    )
    square = jnp.dot(ordered, value, precision=highest, preferred_element_type=jnp.float32)
    gram = slice(widths[0], widths[0] + rank)
    sums[0][:, gram] = square if first else sums_in[0][:, gram] + square
    high, low = split(ordered)
    stacked = jnp.concatenate([high, low], axis=0)

    def part(h, l):
        i = pl.program_id(0)
        both = mul(stacked, h[...])
        product = both[:rank] + (both[rank:] + mul(high, l[...]))
        before = 0
        for s, width in enumerate(widths):

            @pl.when((i >= before // step) & (i < (before + width) // step))
            def _(s=s, before=before):
                at = pl.ds(pl.multiple_of((i - before // step) * step, 128), step)
                sums[s][:, at] = product if first else sums_in[s][:, at] + product

            before += width

    at = pl.ds(start, rows)
    pltpu.emit_pipeline(
        part, grid=(sum(widths) // step,), in_specs=[pl.BlockSpec((rows, step), lambda i: (0, i))] * 2
    )(high_in.at[at], low_in.at[at])


def project(place, start, mine, theirs, halves, before, sums, widths):
    rows, rank = sum(x.shape[0] for x in mine), mine[0].shape[1]
    first = sums is None
    step = largest_divisor(math.gcd(*widths), 640, 128)
    operands = (place, *map(in_hbm, halves), before, *mine, *theirs) + (() if first else tuple(sums))
    specs = [SMEM, ANY, ANY, ANY] + [VMEM] * (len(operands) - 4)
    shapes = [jax.ShapeDtypeStruct((rows, rank), jnp.float32)]
    for s, width in enumerate(widths):
        shapes.append(jax.ShapeDtypeStruct((rank, width + (0 if s else rank)), jnp.float32))
    offset = 4 + 2 * len(mine)
    out = pl.pallas_call(
        functools.partial(project_kernel, start, widths, step, first, len(mine)),
        out_shape=shapes,
        in_specs=specs,
        out_specs=[VMEM] * len(shapes),
        input_output_aliases={} if first else {offset + i: 1 + i for i in range(len(sums))},
        scratch_shapes=[pltpu.VMEM((rank, rows), jnp.float32)],
        compiler_params=pltpu.CompilerParams(vmem_limit_bytes=20 * MIB),
        cost_estimate=cost(1 + rows / 120),
        name="turned_product",
    )(*operands)
    return out[0], list(out[1:])


def inverse_factor_kernel(size, panel, lanes, place, own, other, before, out):
    gram = slice(own.shape[1] - size, own.shape[1])
    block = size // 8
    for r in range(8):
        start = (r % 4) * block
        at = pl.ds(pl.multiple_of((place[0] ^ r) * block, block), block)
        out[at, :] = (own if r < 4 else other)[start : start + block, gram]
    sub = lax.broadcasted_iota(jnp.int32, (panel, lanes), 0)
    lane = lax.broadcasted_iota(jnp.int32, (panel, lanes), 1)
    for j in range(0, size, panel):
        parts = [out[j : j + panel, c : c + lanes] for c in range(0, size, lanes)]
        home, at = divmod(j, lanes)
        columns = [
            jnp.broadcast_to(parts[home][:, at + q : at + q + 1], (panel, lanes)) for q in range(panel)
        ]
        inside = (lane >= at) & (lane < at + panel)
        parts[home] = jnp.where(inside, jnp.where(lane - at == sub, 1.0, 0.0), parts[home])
        for k in range(panel):
            scale = lax.rsqrt(columns[k][k : k + 1, :])
            below = jnp.where(sub > k, columns[k] * scale, 0.0)
            for q in range(k + 1, panel):
                columns[q] = columns[q] - below * (columns[q][k : k + 1, :] * scale)
            for c in range(len(parts)):
                row = parts[c][k : k + 1, :] * scale
                parts[c] = jnp.where(sub == k, row, parts[c] - below * row)
        whole = jnp.concatenate(parts, axis=1)
        out[j : j + panel, :] = whole
        after = j + panel
        if after < size:
            wide = lax.broadcasted_iota(jnp.int32, (panel, size), 1)
            factors = jnp.where(wide >= after, whole, 0.0)
            base = after // lanes * lanes
            change = lax.dot_general(
                factors[:, base:], whole, TRANSPOSED, precision=highest, preferred_element_type=jnp.float32
            )
            rest = out[after:, :]
            column = lax.broadcasted_iota(jnp.int32, rest.shape, 1)
            rest = jnp.where((column >= j) & (column < after), 0.0, rest)
            out[after:, :] = rest - change[after - base :, :]
    row = lax.broadcasted_iota(jnp.int32, (size, size), 0)
    column = lax.broadcasted_iota(jnp.int32, (size, size), 1)
    out[...] = jnp.where(column <= row, out[...], 0.0)


def inverse_factor(place, own, other, before):
    size = 2 * own.shape[0]
    return pl.pallas_call(
        functools.partial(inverse_factor_kernel, size, 16, 128),
        out_shape=jax.ShapeDtypeStruct((size, size), jnp.float32),
        in_specs=[SMEM, VMEM, VMEM, ANY],
        out_specs=VMEM,
        compiler_params=pltpu.CompilerParams(vmem_limit_bytes=8 * MIB),
        cost_estimate=cost(11),
        name="inverse_factor",
    )(place, own, other, before)


def right_kernel(place, own, other, back, out, squares, ordered):
    rank, columns = out.shape
    block = rank // 8
    for r in range(8):
        source = own if r < 4 else other
        start = (r % 4) * block
        at = pl.ds(pl.multiple_of((place[0] ^ r) * block, block), block)
        ordered[at, :] = source[start : start + block, :columns]
    b_high, b_low = split(back[...])
    o_high, o_low = split(ordered[...])
    value = mul(b_high, o_high) + (mul(b_high, o_low) + mul(b_low, o_high))
    out[...] = value
    total = jnp.sum(value * value, axis=1, keepdims=True)
    squares[...] = jnp.broadcast_to(total, (rank, 128)).T[:8, :]


def right_part(place, own, other, back, columns):
    rank = back.shape[0]
    return pl.pallas_call(
        right_kernel,
        out_shape=[
            jax.ShapeDtypeStruct((rank, columns), jnp.float32),
            jax.ShapeDtypeStruct((8, rank), jnp.float32),
        ],
        in_specs=[SMEM, VMEM, VMEM, VMEM],
        out_specs=[VMEM] * 2,
        scratch_shapes=[pltpu.VMEM((rank, columns), jnp.float32)],
        compiler_params=pltpu.CompilerParams(vmem_limit_bytes=16 * MIB),
        cost_estimate=cost(2),
        name="right_columns",
    )(place, own, other, back)


def ortho_kernel(back, proj, out):
    turned_high, turned_low = split(back[...].T)
    high, low = split(proj[...])
    out[...] = mul(high, turned_high) + (mul(high, turned_low) + mul(low, turned_high))


def make_ortho(back, proj):
    rows, rank = proj.shape
    tile = largest_divisor(rows, 400, 16)
    return pl.pallas_call(
        ortho_kernel,
        out_shape=pltpu.HBM((rows, rank), jnp.float32),
        grid=(rows // tile,),
        in_specs=[pl.BlockSpec((rank, rank), lambda i: (0, 0)), pl.BlockSpec((tile, rank), lambda i: (i, 0))],
        out_specs=pl.BlockSpec((tile, rank), lambda i: (i, 0)),
        compiler_params=pltpu.CompilerParams(vmem_limit_bytes=16 * MIB),
        cost_estimate=cost(2),
        name="ortho",
    )(back, proj)


def momentum_kernel(tile, widths, ortho, high_in, low_in, *refs):
    rights, (new_momentum, highs) = refs[: len(widths)], refs[len(widths) :]
    rows, columns = new_momentum.shape
    base = 0
    for width, right in zip(widths, rights):
        highs[:, base : base + width] = right[...].astype(jnp.bfloat16)
        base += width
    step_columns = largest_divisor(columns, 512, 128)

    def step(o, h, l, out):
        high = o[...].astype(jnp.bfloat16)
        for c in range(0, columns, step_columns):
            part = slice(c, c + step_columns)
            old = h[:, part].astype(jnp.float32) + l[:, part].astype(jnp.float32)
            out[:, part] = old - feedback_share * mul(high, highs[:, part])

    wide = pl.BlockSpec((tile, columns), lambda i: (i, 0))
    thin = pl.BlockSpec((tile, ortho.shape[1]), lambda i: (i, 0))
    pltpu.emit_pipeline(step, grid=(rows // tile,), in_specs=[thin, wide, wide], out_specs=[wide])(
        ortho, high_in, low_in, new_momentum
    )


def make_momentum(ortho, halves, rights, widths):
    rows, rank = ortho.shape
    columns = sum(widths)
    tile = largest_divisor(rows, 320, 16)
    return pl.pallas_call(
        functools.partial(momentum_kernel, tile, widths),
        out_shape=pltpu.HBM((rows, columns), jnp.float32),
        in_specs=[ANY, ANY, ANY] + [VMEM] * len(widths),
        out_specs=ANY,
        scratch_shapes=[pltpu.VMEM((rank, columns), jnp.bfloat16)],
        compiler_params=pltpu.CompilerParams(vmem_limit_bytes=30 * MIB),
        cost_estimate=cost(10),
        name="new_momentum",
    )(in_hbm(ortho), *map(in_hbm, halves), *rights)


def weight_kernel(tile, widths, factor, squares, ortho, weight, *refs):
    count = len(widths)
    rights, (new_weight, highs, lows) = refs[:count], refs[count:]
    rows, columns = weight.shape
    scale = factor / jnp.sqrt(squares[0:1, :] + epsilon)
    base = 0
    for width, right in zip(widths, rights):
        highs[:, base : base + width], lows[:, base : base + width] = split(right[...])
        base += width
    step_columns = largest_divisor(columns, 512, 128)

    def step(o, old, out):
        s_high, s_low = split(o[...] * scale)
        stacked = jnp.concatenate([s_high, s_low], axis=0)
        for c in range(0, columns, step_columns):
            part = slice(c, c + step_columns)
            both = mul(stacked, highs[:, part])
            update = both[:tile] + (both[tile:] + mul(s_high, lows[:, part]))
            out[:, part] = decay_keep * old[:, part] - update

    wide = pl.BlockSpec((tile, columns), lambda i: (i, 0))
    thin = pl.BlockSpec((tile, ortho.shape[1]), lambda i: (i, 0))
    pltpu.emit_pipeline(step, grid=(rows // tile,), in_specs=[thin, wide], out_specs=[wide])(
        ortho, weight, new_weight
    )


def make_weight(factor, squares, weight, ortho, rights, widths):
    tile = largest_divisor(weight.shape[0], 320, 16)
    rank = ortho.shape[1]
    return pl.pallas_call(
        functools.partial(weight_kernel, tile, widths, factor),
        out_shape=pltpu.HBM(weight.shape, jnp.float32),
        in_specs=[VMEM, ANY, ANY] + [VMEM] * len(widths),
        out_specs=ANY,
        scratch_shapes=[pltpu.VMEM((rank, sum(widths)), jnp.bfloat16)] * 2,
        compiler_params=pltpu.CompilerParams(vmem_limit_bytes=32 * MIB),
        cost_estimate=cost(10),
        name="new_weight",
    )(squares, in_hbm(ortho), in_hbm(weight), *rights)


def swap_pairs(x, axis, count, stride):
    return lax.ppermute(x, axis, [(i, i ^ stride) for i in range(count)])


def halving_works(count):
    return count >= 8 and count & (count - 1) == 0


def add_after(x, y, before):
    def kernel(x, y, before, out):
        out[...] = x[...] + y[...]

    return pl.pallas_call(
        kernel,
        out_shape=jax.ShapeDtypeStruct(x.shape, x.dtype),
        in_specs=[VMEM, VMEM, ANY],
        out_specs=VMEM,
        compiler_params=pltpu.CompilerParams(vmem_limit_bytes=8 * MIB),
        cost_estimate=cost(0.3),
        name="add_pieces",
    )(x, y, before)


def join_after(pieces, before):
    size = pieces[0].shape[0]

    def kernel(*refs):
        for i in range(len(pieces)):
            refs[-1][i * size : (i + 1) * size, :] = refs[i][...]

    return pl.pallas_call(
        kernel,
        out_shape=jax.ShapeDtypeStruct((len(pieces) * size, pieces[0].shape[1]), pieces[0].dtype),
        in_specs=[VMEM] * len(pieces) + [ANY],
        out_specs=VMEM,
        compiler_params=pltpu.CompilerParams(vmem_limit_bytes=8 * MIB),
        cost_estimate=cost(0.5),
        name="join_pieces",
    )(*pieces, before)


def sums_over(parts, axis, count, work):
    if not halving_works(count) or len(parts) != 2:
        half = parts[0].shape[0] // 2
        totals = [lax.psum(x, axis) for x in parts]
        totals = [(x[:half], x[half:]) for x in totals]
        return totals, work(*totals[0], totals[-1][0])
    pieces = []
    for piece in parts:
        half = piece.shape[0] // 2
        piece = piece[:half] + swap_pairs(piece[half:], axis, count, 1)
        quarter = half // 4
        sent = [swap_pairs(piece[j * quarter : (j + 1) * quarter], axis, count, s) for j, s in ((2, 2), (3, 6), (1, 4))]
        pieces.append(piece[:quarter] + sent[0] + sent[1] + sent[2])
    first, second = pieces
    stride = 8
    while stride < count:
        first = add_after(first, swap_pairs(first, axis, count, stride), pieces[1])
        second = second + swap_pairs(second, axis, count, stride)
        stride *= 2

    def back(piece, before):
        others = [swap_pairs(piece, axis, count, s) for s in (2, 6, 4)]
        whole = join_after([piece, others[2], others[0], others[1]], before)
        return whole, swap_pairs(whole, axis, count, 1)

    first = back(first, second)
    result = work(*first, second)
    return [first, back(second, result)], result


def row_bounds(rows):
    if rows % (25 * 64):
        return [(0, rows)]
    unit = rows // 25
    counts = [4 * unit, 8 * unit, 9 * unit, 4 * unit]
    return [(sum(counts[:i]), count) for i, count in enumerate(counts)]


def stream_widths(columns):
    if columns % (5 * 128):
        return [columns]
    return [columns // 5 * 2, columns // 5 * 3]


def on_device(mesh, weight, grad, momentum, right_factor):
    row_count, col_count = mesh.shape["row"], mesh.shape["col"]
    rows, columns = weight.shape
    rank = right_factor.shape[1]
    bounds = row_bounds(rows)
    widths = stream_widths(columns)
    index = lax.axis_index("row")
    place = jnp.zeros((1,), jnp.int32)
    if halving_works(row_count):
        place = ((index % 2) * 4 + (index // 2 % 2) * 2 + index // 4 % 2).astype(jnp.int32).reshape(1)
    halves, partials, theirs, projs, sums = None, [], [], [], None
    for i, (start, count) in enumerate(bounds):
        if i == 3:
            proj, sums = project(place, 0, partials[:1], theirs[:1], halves, partials[-1], None, widths)
            projs.append(proj)
        earlier = (theirs[i - 2 : i - 1] if i > 1 else []) + projs
        halves, (partial,) = partial_products(start, [count], momentum, grad, right_factor, halves, *earlier)
        partials.append(partial)
        theirs.append(swap_pairs(partial, "col", 2, 1) if col_count == 2 else lax.psum(partial, "col") - partial)
    for i in range(len(projs), len(bounds)):
        proj, sums = project(
            place, bounds[i][0], [partials[i]], [theirs[i]], halves, partials[-1], sums, widths
        )
        projs.append(proj)
    turned, back = sums_over(sums, "row", row_count, functools.partial(inverse_factor, place))
    ortho = make_ortho(back, jnp.concatenate(projs, axis=0))
    rights, squares = zip(*[right_part(place, *pair, back, width) for pair, width in zip(turned, widths)])
    squares = sum(squares[1:], squares[0])
    if col_count == 2:
        squares = squares + swap_pairs(squares, "col", 2, 1)
    else:
        squares = lax.psum(squares, "col")
    new_momentum = make_momentum(ortho, halves, rights, widths)
    whole_rows, whole_columns = rows * row_count, columns * col_count
    factor = step_rate * (whole_rows * whole_columns / rank) ** 0.5
    new_weight = make_weight(factor, squares, weight, ortho, rights, widths)
    share = columns // row_count
    right = jnp.concatenate(rights, axis=1)
    inverse = 1.0 / jnp.sqrt(squares[0] + epsilon)
    own = lax.dynamic_slice_in_dim(right, index * share, share, 1)
    new_right = (own * inverse[:, None]).astype(jnp.bfloat16).T
    return (new_weight, new_momentum, new_right)


def solution(mesh):
    placed = (P("row", "col"), P("row", "col"), P("row", "col"), P("col", None))
    return jax.shard_map(
        functools.partial(on_device, mesh),
        mesh=mesh,
        in_specs=placed,
        out_specs=(P("row", "col"), P("row", "col"), P(("col", "row"), None)),
        check_vma=False,
    )
```

profile of v0, /device:TPU:0, one launch (start us, length us, event | category | flops | bytes accessed | tf_op | source)
XLA Modules:
  0.0 156.2 jit_solution(16958042901790013613)
XLA Ops:
  1.9 4.1 %partial_proj.4 = (bf16[1600,2560]{1,0:T(8,128)(2,1)}, bf16[1600,2560]{1,0:T(8,128)(2,1)}, f32[256,256]{1,0:T(8,128)}) custom-call(f32[1600,2560]{1,0:T(8,128)} %momentum.7, f32[1600,2560]{1,0:T(8,128)} %grad.7, bf16[2560,256]{1,0:T(8,128)(2,1)S(1)} %copy-done), custom_call_target="tpu_custom_call" | custom-call | flops 2951680000 | tf_op jit(solution)/shard_map/partial_proj/pallas_call | solution.py:79
  6.1 2.9 %collective-permute-start = (f32[256,256]{1,0:T(8,128)}, f32[256,256]{1,0:T(8,128)S(1)}, u32[]{:S(2)}, u32[]{:S(2)}) collective-permute-start(f32[256,256]{1,0:T(8,128)} %get-tuple-element.35.refs_0_), channel_id=1, source_target_pairs={{0,1},{1,0},{2,3},{3,2},{4,5},{5,4},{6,7},{7,6},{8,9},{9,8},{10,11... | collective-permute-start | bytes 786440 | tf_op jit(solution)/shard_map/ppermute | solution.py:351
  9.0 7.5 %partial_proj.5 = (bf16[1600,2560]{1,0:T(8,128)(2,1)}, bf16[1600,2560]{1,0:T(8,128)(2,1)}, f32[512,256]{1,0:T(8,128)}) custom-call(f32[1600,2560]{1,0:T(8,128)} %momentum.7, f32[1600,2560]{1,0:T(8,128)} %grad.7, bf16[2560,256]{1,0:T(8,128)(2,1)S(1)} %copy-done, ...), custom_call_target="tpu_custom_call", output_to_operand_aliasing={{0}: (3, {}), {1}: (4, {})} | custom-call | flops 5903360000 | tf_op jit(solution)/shard_map/partial_proj/pallas_call | solution.py:79
  16.6 8.7 %partial_proj.6 = (bf16[1600,2560]{1,0:T(8,128)(2,1)}, bf16[1600,2560]{1,0:T(8,128)(2,1)}, f32[576,256]{1,0:T(8,128)}) custom-call(f32[1600,2560]{1,0:T(8,128)} %momentum.7, f32[1600,2560]{1,0:T(8,128)} %grad.7, bf16[2560,256]{1,0:T(8,128)(2,1)S(1)} %copy-done.1, ...), custom_call_target="tpu_custom_call", output_to_operand_aliasing={{0}: (3, {}), {1}: (4, {})} | custom-call | flops 6641280000 | tf_op jit(solution)/shard_map/partial_proj/pallas_call | solution.py:79
  25.3 2.0 %collective-permute-start.3 = (f32[576,256]{1,0:T(8,128)}, f32[576,256]{1,0:T(8,128)S(1)}, u32[]{:S(2)}, u32[]{:S(2)}) collective-permute-start(f32[576,256]{1,0:T(8,128)} %get-tuple-element.39.before.refs_0_), channel_id=1, source_target_pairs={{0,1},{1,0},{2,3},{3,2},{4,5},{5,4},{6,7},{7,6},{8,9},{9,8},{10,11... | collective-permute-start | bytes 1769480 | tf_op jit(solution)/shard_map/ppermute | solution.py:351
  28.4 4.9 %turned_product.4 = (f32[256,256]{1,0:T(8,128)S(1)}, f32[256,1280]{1,0:T(8,128)S(1)}, f32[256,1536]{1,0:T(8,128)S(1)}) custom-call(s32[1]{0:T(128)} %bitcast.place, bf16[1600,2560]{1,0:T(8,128)(2,1)} %get-tuple-element.36.high_in.refs_0_, bf16[1600,2560]{1,0:T(8,128)(2,1)} %get-tuple-element.37.low_in.refs_1_, f32[576,256]{1,0:T(8,128)S(1)} %copy-done.4, ...), custom_call_target="tpu_custom_call" | custom-call | flops 3612733440 | tf_op jit(solution)/shard_map/turned_product/pallas_call | solution.py:144
  33.3 4.2 %partial_proj.7 = (bf16[1600,2560]{1,0:T(8,128)(2,1)}, bf16[1600,2560]{1,0:T(8,128)(2,1)}, f32[256,256]{1,0:T(8,128)}) custom-call(f32[1600,2560]{1,0:T(8,128)} %momentum.7, f32[1600,2560]{1,0:T(8,128)} %grad.7, bf16[2560,256]{1,0:T(8,128)(2,1)S(1)} %copy-done.1, ...), custom_call_target="tpu_custom_call", output_to_operand_aliasing={{0}: (3, {}), {1}: (4, {})} | custom-call | flops 2951680000 | tf_op jit(solution)/shard_map/partial_proj/pallas_call | solution.py:79
  38.5 6.7 %turned_product.5 = (f32[512,256]{1,0:T(8,128)S(1)}, f32[256,1280]{1,0:T(8,128)S(1)}, f32[256,1536]{1,0:T(8,128)S(1)}) custom-call(s32[1]{0:T(128)} %bitcast.place, bf16[1600,2560]{1,0:T(8,128)(2,1)} %get-tuple-element.41.high_in, bf16[1600,2560]{1,0:T(8,128)(2,1)} %get-tuple-element.42.low_in, ...), custom_call_target="tpu_custom_call", output_to_operand_aliasing={{1}: (6, {}), {2}: (7, {})} | custom-call | flops 6072466432 | tf_op jit(solution)/shard_map/turned_product/pallas_call | solution.py:144
  45.3 7.6 %turned_product.6 = (f32[576,256]{1,0:T(8,128)S(1)}, f32[256,1280]{1,0:T(8,128)S(1)}, f32[256,1536]{1,0:T(8,128)S(1)}) custom-call(s32[1]{0:T(128)} %bitcast.place, bf16[1600,2560]{1,0:T(8,128)(2,1)} %get-tuple-element.41.high_in, bf16[1600,2560]{1,0:T(8,128)(2,1)} %get-tuple-element.42.low_in, ...), custom_call_target="tpu_custom_call", output_to_operand_aliasing={{1}: (6, {}), {2}: (7, {})} | custom-call | flops 6687399936 | tf_op jit(solution)/shard_map/turned_product/pallas_call | solution.py:144
  52.9 5.3 %turned_product.7 = (f32[256,256]{1,0:T(8,128)S(1)}, f32[256,1280]{1,0:T(8,128)S(1)}, f32[256,1536]{1,0:T(8,128)S(1)}) custom-call(s32[1]{0:T(128)} %bitcast.place, bf16[1600,2560]{1,0:T(8,128)(2,1)} %get-tuple-element.41.high_in, bf16[1600,2560]{1,0:T(8,128)(2,1)} %get-tuple-element.42.low_in, ...), custom_call_target="tpu_custom_call", output_to_operand_aliasing={{1}: (6, {}), {2}: (7, {})} | custom-call | flops 3612733440 | tf_op jit(solution)/shard_map/turned_product/pallas_call | solution.py:144
  60.6 2.1 %collective-permute-start.5 = (f32[32,1280]{1,0:T(8,128)S(1)}, f32[32,1280]{1,0:T(8,128)S(1)}, u32[]{:S(2)}, u32[]{:S(2)}) collective-permute-start(f32[32,1280]{1,0:T(8,128)S(1)} %get-tuple-element.65), channel_id=1, source_target_pairs={{0,4},{2,6},{4,0},{6,2},{8,12},{10,14},{12,8},{14,10},{16,20},{18,... | collective-permute-start | bytes 491528 | tf_op jit(solution)/shard_map/ppermute | solution.py:351
  62.7 1.5 collective-permute-start.6
  64.5 2.0 %collective-permute-start.10 = (f32[32,1536]{1,0:T(8,128)S(1)}, f32[32,1536]{1,0:T(8,128)S(1)}, u32[]{:S(2)}, u32[]{:S(2)}) collective-permute-start(f32[32,1536]{1,0:T(8,128)S(1)} %get-tuple-element.62), channel_id=1, source_target_pairs={{0,4},{2,6},{4,0},{6,2},{8,12},{10,14},{12,8},{14,10},{16,20},{18,... | collective-permute-start | bytes 589832 | tf_op jit(solution)/shard_map/ppermute | solution.py:351
  66.4 1.5 collective-permute-start.11
  67.9 3.3 %collective-permute-done.5 = f32[32,1280]{1,0:T(8,128)S(1)} collective-permute-done((f32[32,1280]{1,0:T(8,128)S(1)}, f32[32,1280]{1,0:T(8,128)S(1)}, u32[]{:S(2)}, u32[]{:S(2)}) %collective-permute-start.5) | collective-permute-done | bytes 163872 | tf_op jit(solution)/shard_map/ppermute | solution.py:351
  71.2 2.1 %collective-permute-start.12 = (f32[32,1536]{1,0:T(8,128)S(1)}, f32[32,1536]{1,0:T(8,128)S(1)}, u32[]{:S(2)}, u32[]{:S(2)}) collective-permute-start(f32[32,1536]{1,0:T(8,128)S(1)} %get-tuple-element.63), channel_id=1, source_target_pairs={{0,8},{2,10},{4,12},{6,14},{8,0},{10,2},{12,4},{14,6},{16,24},{18,... | collective-permute-start | bytes 589832 | tf_op jit(solution)/shard_map/ppermute | solution.py:351
  73.4 2.7 %collective-permute-start.8 = (f32[32,1280]{1,0:T(8,128)S(1)}, f32[32,1280]{1,0:T(8,128)S(1)}, u32[]{:S(2)}, u32[]{:S(2)}) collective-permute-start(f32[32,1280]{1,0:T(8,128)S(1)} %fusion.6.x), channel_id=1, source_target_pairs={{0,16},{2,18},{4,20},{6,22},{8,24},{10,26},{12,28},{14,30},{16,0},... | collective-permute-start | bytes 491528 | tf_op jit(solution)/shard_map/ppermute | solution.py:351
  76.0 2.0 %collective-permute-done.10 = f32[32,1536]{1,0:T(8,128)S(1)} collective-permute-done((f32[32,1536]{1,0:T(8,128)S(1)}, f32[32,1536]{1,0:T(8,128)S(1)}, u32[]{:S(2)}, u32[]{:S(2)}) %collective-permute-start.10) | collective-permute-done | bytes 196640 | tf_op jit(solution)/shard_map/ppermute | solution.py:351
  78.0 4.0 %collective-permute-done.11 = f32[32,1536]{1,0:T(8,128)S(1)} collective-permute-done((f32[32,1536]{1,0:T(8,128)S(1)}, f32[32,1536]{1,0:T(8,128)S(1)}, u32[]{:S(2)}, u32[]{:S(2)}) %collective-permute-start.11) | collective-permute-done | bytes 196640 | tf_op jit(solution)/shard_map/ppermute | solution.py:351
  82.0 2.1 %collective-permute-done.12 = f32[32,1536]{1,0:T(8,128)S(1)} collective-permute-done((f32[32,1536]{1,0:T(8,128)S(1)}, f32[32,1536]{1,0:T(8,128)S(1)}, u32[]{:S(2)}, u32[]{:S(2)}) %collective-permute-start.12) | collective-permute-done | bytes 196640 | tf_op jit(solution)/shard_map/ppermute | solution.py:351
  84.1 1.9 %collective-permute-start.16 = (f32[32,1536]{1,0:T(8,128)S(1)}, f32[32,1536]{1,0:T(8,128)S(1)}, u32[]{:S(2)}, u32[]{:S(2)}) collective-permute-start(f32[32,1536]{1,0:T(8,128)S(1)} %fusion.4.before), channel_id=1, source_target_pairs={{0,16},{2,18},{4,20},{6,22},{8,24},{10,26},{12,28},{14,30},{16,0},... | collective-permute-start | bytes 589832 | tf_op jit(solution)/shard_map/ppermute | solution.py:351
  86.0 2.5 %collective-permute-start.13 = (f32[32,1280]{1,0:T(8,128)S(1)}, f32[32,1280]{1,0:T(8,128)S(1)}, u32[]{:S(2)}, u32[]{:S(2)}) collective-permute-start(f32[32,1280]{1,0:T(8,128)S(1)} %add_pieces.1.refs_0_), channel_id=1, source_target_pairs={{0,8},{2,10},{4,12},{6,14},{8,0},{10,2},{12,4},{14,6},{16,24},{18,... | collective-permute-start | bytes 491528 | tf_op jit(solution)/shard_map/ppermute | solution.py:351
  88.5 1.5 collective-permute-start.14
  90.1 5.4 %collective-permute-done.16 = f32[32,1536]{1,0:T(8,128)S(1)} collective-permute-done((f32[32,1536]{1,0:T(8,128)S(1)}, f32[32,1536]{1,0:T(8,128)S(1)}, u32[]{:S(2)}, u32[]{:S(2)}) %collective-permute-start.16) | collective-permute-done | bytes 196640 | tf_op jit(solution)/shard_map/ppermute | solution.py:351
  96.4 3.0 %collective-permute-done.15.refs_3_ = f32[32,1280]{1,0:T(8,128)S(1)} collective-permute-done((f32[32,1280]{1,0:T(8,128)S(1)}, f32[32,1280]{1,0:T(8,128)S(1)}, u32[]{:S(2)}, u32[]{:S(2)}) %collective-permute-start.15) | collective-permute-done | bytes 163872 | tf_op jit(solution)/shard_map/ppermute | solution.py:351
  100.5 2.6 %collective-permute-start.20 = (f32[32,1536]{1,0:T(8,128)S(1)}, f32[32,1536]{1,0:T(8,128)S(1)}, u32[]{:S(2)}, u32[]{:S(2)}) collective-permute-start(f32[32,1536]{1,0:T(8,128)S(1)} %add.78.refs_4_.before.refs_0_), channel_id=1, source_target_pairs={{0,12},{2,14},{4,8},{6,10},{8,4},{10,6},{12,0},{14,2},{16,28},{18,... | collective-permute-start | bytes 589832 | tf_op jit(solution)/shard_map/ppermute | solution.py:351
  103.2 10.7 %inverse_factor.1.back.refs_4_ = f32[256,256]{1,0:T(8,128)S(1)} custom-call(s32[1]{0:T(128)} %bitcast.place, f32[128,1280]{1,0:T(8,128)S(1)} %join_pieces.2.own, f32[128,1280]{1,0:T(8,128)S(1)} %collective-permute-done.17.other, f32[32,1536]{1,0:T(8,128)S(1)} %add.78.refs_4_.before.refs_0_), custom_call_target="tpu_custom_call" | custom-call | flops 12682999808 | tf_op jit(solution)/shard_map/inverse_factor/pallas_call | solution.py:204
  114.6 2.9 %ortho.1 = f32[1600,256]{1,0:T(8,128)} custom-call(f32[256,256]{1,0:T(8,128)S(1)} %inverse_factor.1.back.refs_4_, f32[1600,256]{1,0:T(8,128)S(1)} %pad_maximum_fusion.proj), custom_call_target="tpu_custom_call" | custom-call | flops 2305999872 | tf_op jit(solution)/shard_map/ortho/pallas_call | solution.py:257
  119.4 2.1 %right_columns.3 = (f32[256,1536]{1,0:T(8,128)S(1)}, f32[8,256]{1,0:T(8,128)S(1)}) custom-call(s32[1]{0:T(128)} %bitcast.place, f32[128,1536]{1,0:T(8,128)S(1)} %join_pieces.3.own, f32[128,1536]{1,0:T(8,128)} %collective-permute-done.21.other, f32[256,256]{1,0:T(8,128)S(1)} %copy-done.14), custom_call_target="tpu_custom_call" | custom-call | flops 2305999872 | tf_op jit(solution)/shard_map/right_columns/pallas_call | solution.py:233
  121.6 1.5 collective-permute-start.22
  123.1 14.9 %new_momentum.1 = f32[1600,2560]{1,0:T(8,128)} custom-call(f32[1600,256]{1,0:T(8,128)} %ortho.1, bf16[1600,2560]{1,0:T(8,128)(2,1)} %get-tuple-element.41.high_in, bf16[1600,2560]{1,0:T(8,128)(2,1)} %get-tuple-element.42.low_in, f32[256,1024]{1,0:T(8,128)S(1)} %get-tuple-element.57.refs_0_, f32[256,1536]{1,0:T(8,128)S(1)} %get-tuple-element.58.refs_1_), custom_call_target="tpu_custom_call" | custom-call | flops 11530000384 | tf_op jit(solution)/shard_map/new_momentum/pallas_call | solution.py:296
  139.0 17.2 %new_weight.1 = f32[1600,2560]{1,0:T(8,128)} custom-call(f32[8,256]{1,0:T(8,128)S(1)} %add.80.squares, f32[1600,256]{1,0:T(8,128)} %ortho.1, f32[1600,2560]{1,0:T(8,128)} %weight.1, f32[256,1024]{1,0:T(8,128)S(1)} %get-tuple-element.57.refs_0_, f32[256,1536]{1,0:T(8,128)S(1)} %get-tuple-element.58.refs_1_), custom_call_target="tpu_custom_call" | custom-call | flops 11530000384 | tf_op jit(solution)/shard_map/new_weight/pallas_call | solution.py:338
  (76 shorter events, 11.7 us)
Async XLA Ops:
  6.1 10.5 %collective-permute-start = (f32[256,256]{1,0:T(8,128)}, f32[256,256]{1,0:T(8,128)S(1)}, u32[]{:S(2)}, u32[]{:S(2)}) collective-permute-start(f32[256,256]{1,0:T(8,128)} %get-tuple-element.35.refs_0_), channel_id=1, source_target_pairs={{0,1},{1,0},{2,3},{3,2},{4,5},{5,4},{6,7},{7,6},{8,9},{9,8},{10,11... | collective-permute-start | bytes 786440 | tf_op jit(solution)/shard_map/ppermute | solution.py:351
  9.0 7.5 %copy-start.1 = (bf16[2560,256]{1,0:T(8,128)(2,1)S(1)}, bf16[2560,256]{1,0:T(8,128)(2,1)}, u32[]{:S(2)}) copy-start(bf16[2560,256]{1,0:T(8,128)(2,1)} %right_factor.7) | copy-start | bytes 3932164
  16.5 16.8 %collective-permute-start.1 = (f32[512,256]{1,0:T(8,128)}, f32[512,256]{1,0:T(8,128)S(1)}, u32[]{:S(2)}, u32[]{:S(2)}) collective-permute-start(f32[512,256]{1,0:T(8,128)} %get-tuple-element.38.refs_0_), channel_id=1, source_target_pairs={{0,1},{1,0},{2,3},{3,2},{4,5},{5,4},{6,7},{7,6},{8,9},{9,8},{10,11... | collective-permute-start | bytes 1572872 | tf_op jit(solution)/shard_map/ppermute | solution.py:351
  16.5 10.7 %copy-start.6 = (f32[256,256]{1,0:T(8,128)S(1)}, f32[256,256]{1,0:T(8,128)}, u32[]{:S(2)}) copy-start(f32[256,256]{1,0:T(8,128)} %get-tuple-element.35.refs_0_) | copy-start | bytes 786436
  25.3 20.0 %collective-permute-start.3 = (f32[576,256]{1,0:T(8,128)}, f32[576,256]{1,0:T(8,128)S(1)}, u32[]{:S(2)}, u32[]{:S(2)}) collective-permute-start(f32[576,256]{1,0:T(8,128)} %get-tuple-element.39.before.refs_0_), channel_id=1, source_target_pairs={{0,1},{1,0},{2,3},{3,2},{4,5},{5,4},{6,7},{7,6},{8,9},{9,8},{10,11... | collective-permute-start | bytes 1769480 | tf_op jit(solution)/shard_map/ppermute | solution.py:351
  33.3 4.2 %copy-start.11 = (f32[512,256]{1,0:T(8,128)S(1)}, f32[512,256]{1,0:T(8,128)}, u32[]{:S(2)}) copy-start(f32[512,256]{1,0:T(8,128)} %get-tuple-element.38.refs_0_) | copy-start | bytes 1572868
  37.5 15.4 %collective-permute-start.2 = (f32[256,256]{1,0:T(8,128)}, f32[256,256]{1,0:T(8,128)S(1)}, u32[]{:S(2)}, u32[]{:S(2)}) collective-permute-start(f32[256,256]{1,0:T(8,128)} %get-tuple-element.43.before.refs_0_), channel_id=1, source_target_pairs={{0,1},{1,0},{2,3},{3,2},{4,5},{5,4},{6,7},{7,6},{8,9},{9,8},{10,11... | collective-permute-start | bytes 786440 | tf_op jit(solution)/shard_map/ppermute | solution.py:351
  38.5 6.7 %copy-start.3 = (f32[256,256]{1,0:T(8,128)S(1)}, f32[256,256]{1,0:T(8,128)}, u32[]{:S(2)}) copy-start(f32[256,256]{1,0:T(8,128)} %get-tuple-element.43.before.refs_0_) | copy-start | bytes 786436
  38.5 6.7 %copy-start.5 = (f32[576,256]{1,0:T(8,128)S(1)}, f32[576,256]{1,0:T(8,128)}, u32[]{:S(2)}) copy-start(f32[576,256]{1,0:T(8,128)} %get-tuple-element.39.before.refs_0_) | copy-start | bytes 1769476
  58.3 2.2 %collective-permute-start.4 = (f32[128,1280]{1,0:T(8,128)S(1)}, f32[128,1280]{1,0:T(8,128)S(1)}, u32[]{:S(2)}, u32[]{:S(2)}) collective-permute-start(f32[128,1280]{1,0:T(8,128)S(1)} %slice.40), channel_id=1, source_target_pairs={{0,2},{2,0},{4,6},{6,4},{8,10},{10,8},{12,14},{14,12},{16,18},{18,... | collective-permute-start | bytes 1966088 | tf_op jit(solution)/shard_map/ppermute | solution.py:351
  58.5 5.8 %collective-permute-start.9 = (f32[128,1536]{1,0:T(8,128)S(1)}, f32[128,1536]{1,0:T(8,128)S(1)}, u32[]{:S(2)}, u32[]{:S(2)}) collective-permute-start(f32[128,1536]{1,0:T(8,128)S(1)} %slice.46), channel_id=1, source_target_pairs={{0,2},{2,0},{4,6},{6,4},{8,10},{10,8},{12,14},{14,12},{16,18},{18,... | collective-permute-start | bytes 2359304 | tf_op jit(solution)/shard_map/ppermute | solution.py:351
  60.6 10.6 %collective-permute-start.5 = (f32[32,1280]{1,0:T(8,128)S(1)}, f32[32,1280]{1,0:T(8,128)S(1)}, u32[]{:S(2)}, u32[]{:S(2)}) collective-permute-start(f32[32,1280]{1,0:T(8,128)S(1)} %get-tuple-element.65), channel_id=1, source_target_pairs={{0,4},{2,6},{4,0},{6,2},{8,12},{10,14},{12,8},{14,10},{16,20},{18,... | collective-permute-start | bytes 491528 | tf_op jit(solution)/shard_map/ppermute | solution.py:351
  62.7 10.6 %collective-permute-start.6 = (f32[32,1280]{1,0:T(8,128)S(1)}, f32[32,1280]{1,0:T(8,128)S(1)}, u32[]{:S(2)}, u32[]{:S(2)}) collective-permute-start(f32[32,1280]{1,0:T(8,128)S(1)} %get-tuple-element.67), channel_id=1, source_target_pairs={{0,12},{2,14},{4,8},{6,10},{8,4},{10,6},{12,0},{14,2},{16,28},{18,... | collective-permute-start | bytes 491528 | tf_op jit(solution)/shard_map/ppermute | solution.py:351
  64.2 9.1 %collective-permute-start.7 = (f32[32,1280]{1,0:T(8,128)S(1)}, f32[32,1280]{1,0:T(8,128)S(1)}, u32[]{:S(2)}, u32[]{:S(2)}) collective-permute-start(f32[32,1280]{1,0:T(8,128)S(1)} %get-tuple-element.66), channel_id=1, source_target_pairs={{0,8},{2,10},{4,12},{6,14},{8,0},{10,2},{12,4},{14,6},{16,24},{18,... | collective-permute-start | bytes 491528 | tf_op jit(solution)/shard_map/ppermute | solution.py:351
  64.5 13.5 %collective-permute-start.10 = (f32[32,1536]{1,0:T(8,128)S(1)}, f32[32,1536]{1,0:T(8,128)S(1)}, u32[]{:S(2)}, u32[]{:S(2)}) collective-permute-start(f32[32,1536]{1,0:T(8,128)S(1)} %get-tuple-element.62), channel_id=1, source_target_pairs={{0,4},{2,6},{4,0},{6,2},{8,12},{10,14},{12,8},{14,10},{16,20},{18,... | collective-permute-start | bytes 589832 | tf_op jit(solution)/shard_map/ppermute | solution.py:351
  66.4 15.5 %collective-permute-start.11 = (f32[32,1536]{1,0:T(8,128)S(1)}, f32[32,1536]{1,0:T(8,128)S(1)}, u32[]{:S(2)}, u32[]{:S(2)}) collective-permute-start(f32[32,1536]{1,0:T(8,128)S(1)} %get-tuple-element.64), channel_id=1, source_target_pairs={{0,12},{2,14},{4,8},{6,10},{8,4},{10,6},{12,0},{14,2},{16,28},{18,... | collective-permute-start | bytes 589832 | tf_op jit(solution)/shard_map/ppermute | solution.py:351
  71.2 12.8 %collective-permute-start.12 = (f32[32,1536]{1,0:T(8,128)S(1)}, f32[32,1536]{1,0:T(8,128)S(1)}, u32[]{:S(2)}, u32[]{:S(2)}) collective-permute-start(f32[32,1536]{1,0:T(8,128)S(1)} %get-tuple-element.63), channel_id=1, source_target_pairs={{0,8},{2,10},{4,12},{6,14},{8,0},{10,2},{12,4},{14,6},{16,24},{18,... | collective-permute-start | bytes 589832 | tf_op jit(solution)/shard_map/ppermute | solution.py:351
  73.4 12.6 %collective-permute-start.8 = (f32[32,1280]{1,0:T(8,128)S(1)}, f32[32,1280]{1,0:T(8,128)S(1)}, u32[]{:S(2)}, u32[]{:S(2)}) collective-permute-start(f32[32,1280]{1,0:T(8,128)S(1)} %fusion.6.x), channel_id=1, source_target_pairs={{0,16},{2,18},{4,20},{6,22},{8,24},{10,26},{12,28},{14,30},{16,0},... | collective-permute-start | bytes 491528 | tf_op jit(solution)/shard_map/ppermute | solution.py:351
  84.1 11.4 %collective-permute-start.16 = (f32[32,1536]{1,0:T(8,128)S(1)}, f32[32,1536]{1,0:T(8,128)S(1)}, u32[]{:S(2)}, u32[]{:S(2)}) collective-permute-start(f32[32,1536]{1,0:T(8,128)S(1)} %fusion.4.before), channel_id=1, source_target_pairs={{0,16},{2,18},{4,20},{6,22},{8,24},{10,26},{12,28},{14,30},{16,0},... | collective-permute-start | bytes 589832 | tf_op jit(solution)/shard_map/ppermute | solution.py:351
  86.0 10.4 %collective-permute-start.13 = (f32[32,1280]{1,0:T(8,128)S(1)}, f32[32,1280]{1,0:T(8,128)S(1)}, u32[]{:S(2)}, u32[]{:S(2)}) collective-permute-start(f32[32,1280]{1,0:T(8,128)S(1)} %add_pieces.1.refs_0_), channel_id=1, source_target_pairs={{0,8},{2,10},{4,12},{6,14},{8,0},{10,2},{12,4},{14,6},{16,24},{18,... | collective-permute-start | bytes 491528 | tf_op jit(solution)/shard_map/ppermute | solution.py:351
  88.5 7.9 %collective-permute-start.14 = (f32[32,1280]{1,0:T(8,128)S(1)}, f32[32,1280]{1,0:T(8,128)S(1)}, u32[]{:S(2)}, u32[]{:S(2)}) collective-permute-start(f32[32,1280]{1,0:T(8,128)S(1)} %add_pieces.1.refs_0_), channel_id=1, source_target_pairs={{0,4},{2,6},{4,0},{6,2},{8,12},{10,14},{12,8},{14,10},{16,20},{18,... | collective-permute-start | bytes 491528 | tf_op jit(solution)/shard_map/ppermute | solution.py:351
  90.0 9.4 %collective-permute-start.15 = (f32[32,1280]{1,0:T(8,128)S(1)}, f32[32,1280]{1,0:T(8,128)S(1)}, u32[]{:S(2)}, u32[]{:S(2)}) collective-permute-start(f32[32,1280]{1,0:T(8,128)S(1)} %add_pieces.1.refs_0_), channel_id=1, source_target_pairs={{0,12},{2,14},{4,8},{6,10},{8,4},{10,6},{12,0},{14,2},{16,28},{18,... | collective-permute-start | bytes 491528 | tf_op jit(solution)/shard_map/ppermute | solution.py:351
  99.5 14.4 %copy-start.7 = (f32[128,1280]{1,0:T(8,128)}, f32[128,1280]{1,0:T(8,128)S(1)}, u32[]{:S(2)}) copy-start(f32[128,1280]{1,0:T(8,128)S(1)} %join_pieces.2.own) | copy-start | bytes 1966084
  99.5 3.6 %collective-permute-start.17 = (f32[128,1280]{1,0:T(8,128)S(1)}, f32[128,1280]{1,0:T(8,128)S(1)}, u32[]{:S(2)}, u32[]{:S(2)}) collective-permute-start(f32[128,1280]{1,0:T(8,128)S(1)} %join_pieces.2.own), channel_id=1, source_target_pairs={{0,2},{2,0},{4,6},{6,4},{8,10},{10,8},{12,14},{14,12},{16,18},{18,... | collective-permute-start | bytes 1966088 | tf_op jit(solution)/shard_map/ppermute | solution.py:351
  99.6 14.3 %collective-permute-start.18 = (f32[32,1536]{1,0:T(8,128)S(1)}, f32[32,1536]{1,0:T(8,128)S(1)}, u32[]{:S(2)}, u32[]{:S(2)}) collective-permute-start(f32[32,1536]{1,0:T(8,128)S(1)} %add.78.refs_4_.before.refs_0_), channel_id=1, source_target_pairs={{0,8},{2,10},{4,12},{6,14},{8,0},{10,2},{12,4},{14,6},{16,24},{18,... | collective-permute-start | bytes 589832 | tf_op jit(solution)/shard_map/ppermute | solution.py:351
  100.0 13.9 %collective-permute-start.19 = (f32[32,1536]{1,0:T(8,128)S(1)}, f32[32,1536]{1,0:T(8,128)S(1)}, u32[]{:S(2)}, u32[]{:S(2)}) collective-permute-start(f32[32,1536]{1,0:T(8,128)S(1)} %add.78.refs_4_.before.refs_0_), channel_id=1, source_target_pairs={{0,4},{2,6},{4,0},{6,2},{8,12},{10,14},{12,8},{14,10},{16,20},{18,... | collective-permute-start | bytes 589832 | tf_op jit(solution)/shard_map/ppermute | solution.py:351
  100.5 13.4 %collective-permute-start.20 = (f32[32,1536]{1,0:T(8,128)S(1)}, f32[32,1536]{1,0:T(8,128)S(1)}, u32[]{:S(2)}, u32[]{:S(2)}) collective-permute-start(f32[32,1536]{1,0:T(8,128)S(1)} %add.78.refs_4_.before.refs_0_), channel_id=1, source_target_pairs={{0,12},{2,14},{4,8},{6,10},{8,4},{10,6},{12,0},{14,2},{16,28},{18,... | collective-permute-start | bytes 589832 | tf_op jit(solution)/shard_map/ppermute | solution.py:351
  103.2 10.7 %copy-start.9 = (f32[128,1280]{1,0:T(8,128)}, f32[128,1280]{1,0:T(8,128)S(1)}, u32[]{:S(2)}) copy-start(f32[128,1280]{1,0:T(8,128)S(1)} %collective-permute-done.17.other) | copy-start | bytes 1966084
  114.0 5.3 %collective-permute-start.21 = (f32[128,1536]{1,0:T(8,128)S(1)}, f32[128,1536]{1,0:T(8,128)}, u32[]{:S(2)}, u32[]{:S(2)}) collective-permute-start(f32[128,1536]{1,0:T(8,128)S(1)} %join_pieces.3.own), channel_id=1, source_target_pairs={{0,2},{2,0},{4,6},{6,4},{8,10},{10,8},{12,14},{14,12},{16,18},{18,... | collective-permute-start | bytes 2359304 | tf_op jit(solution)/shard_map/ppermute | solution.py:351
  114.6 2.9 %copy-start.8 = (f32[128,1280]{1,0:T(8,128)S(1)}, f32[128,1280]{1,0:T(8,128)}, u32[]{:S(2)}) copy-start(f32[128,1280]{1,0:T(8,128)} %copy-done.7) | copy-start | bytes 1966084
  114.6 2.9 %copy-start.10 = (f32[128,1280]{1,0:T(8,128)S(1)}, f32[128,1280]{1,0:T(8,128)}, u32[]{:S(2)}) copy-start(f32[128,1280]{1,0:T(8,128)} %copy-done.9) | copy-start | bytes 1966084
  121.6 16.4 %collective-permute-start.22 = (f32[8,256]{1,0:T(8,128)S(1)}, f32[8,256]{1,0:T(8,128)S(1)}, u32[]{:S(2)}, u32[]{:S(2)}) collective-permute-start(f32[8,256]{1,0:T(8,128)S(1)} %add.79), channel_id=1, source_target_pairs={{0,1},{1,0},{2,3},{3,2},{4,5},{5,4},{6,7},{7,6},{8,9},{9,8},{10,11... | collective-permute-start | bytes 24584 | tf_op jit(solution)/shard_map/ppermute | solution.py:351
  (6 other events, 6.0 us)
where the time goes:
time: 157 us; the launch traced here: 156 us
  Pallas kernels  97.8 us (62%)
  starting transfers between devices  28.7 us (18%)
  waiting for transfers between devices  22.1 us (14%)
  local copies, waits for them, and re-layouts  5.92 us (4%)
    ppermute x23, starting transfers between devices, swap_pairs(): return lax.ppermute(x, axis, [(i, i ^ stride) for i in range(count)])  28.7 us
    pallas_call x4, Pallas kernels, project(): pl.pallas_call(functools.partial(project_kernel, start, widths, step, fir...  24.6 us
    pallas_call x4, Pallas kernels, partial_products(): pl.pallas_call(functools.partial(partial_kernel, start, counts, tile), ou...  24.6 us
    ppermute x23, waiting for transfers between devices, swap_pairs(): return lax.ppermute(x, axis, [(i, i ^ stride) for i in range(count)])  22.1 us
    pallas_call x1, Pallas kernels, make_weight(): pl.pallas_call(functools.partial(weight_kernel, tile, widths, factor), ou...  17.2 us
    pallas_call x1, Pallas kernels, make_momentum(): pl.pallas_call(functools.partial(momentum_kernel, tile, widths), out_shap...  14.9 us
    pallas_call x1, Pallas kernels, inverse_factor(): pl.pallas_call(functools.partial(inverse_factor_kernel, size, 16, 128), o...  10.7 us
    unnamed x31, local copies, waits for them, and re-layouts  5.75 us
  transfers between devices with their start and end apart: 23, of which 8 were waited for; matrix products, arithmetic and copies ran while one was open for 0% of the time, Pallas kernels for 44%

commit v1 on v0

--- a/solution.py
+++ b/solution.py
@@ -50,13 +50,20 @@
 
 def partial_kernel(start, counts, tile, momentum, grad, right_factor, *refs):
     count = len(counts)
-    high_out, low_out, *partials = refs[-2 - count :]
+    high_out, low_out, *partials = refs[-4 - count : -2]
+    factor, arrived = refs[-2:]
+    copy = pltpu.make_async_copy(right_factor, factor, arrived)
+    copy.start()
 
     def step(m, g, h, l, out):
+        @pl.when(pl.program_id(0) == 0)
+        def _():
+            copy.wait()
+
         high, low = split(m[...] + g[...])
         h[...] = high
         l[...] = low
-        both = mul(jnp.concatenate([high, low], axis=0), right_factor[...])
+        both = mul(jnp.concatenate([high, low], axis=0), factor[...])
         out[...] = both[:tile] + both[tile:]
 
     columns = momentum.shape[1]
@@ -79,13 +86,14 @@
     out = pl.pallas_call(
         functools.partial(partial_kernel, start, counts, tile),
         out_shape=shapes,
-        in_specs=[ANY, ANY, VMEM] + [ANY] * (len(halves) + len(earlier)),
+        in_specs=[ANY] * (3 + len(halves) + len(earlier)),
         out_specs=[ANY] * len(shapes),
+        scratch_shapes=[pltpu.VMEM((columns, rank), right_factor.dtype), pltpu.SemaphoreType.DMA],
         input_output_aliases={3 + i: i for i in range(len(halves))},
         compiler_params=pltpu.CompilerParams(vmem_limit_bytes=16 * MIB),
         cost_estimate=cost(sum(counts) / 100),
         name="partial_proj",
-    )(in_hbm(momentum), in_hbm(grad), right_factor, *halves, *earlier)
+    )(in_hbm(momentum), in_hbm(grad), in_hbm(right_factor), *halves, *earlier)
     return out[:2], out[2:]
 
 
@@ -267,7 +275,7 @@
 
 
 def momentum_kernel(tile, widths, ortho, high_in, low_in, *refs):
-    rights, (new_momentum, highs) = refs[: len(widths)], refs[len(widths) :]
+    rights, (before, new_momentum, highs) = refs[: len(widths)], refs[len(widths) :]
     rows, columns = new_momentum.shape
     base = 0
     for width, right in zip(widths, rights):
@@ -289,20 +297,20 @@
     )
 
 
-def make_momentum(ortho, halves, rights, widths):
+def make_momentum(ortho, halves, rights, widths, before):
     rows, rank = ortho.shape
     columns = sum(widths)
     tile = largest_divisor(rows, 320, 16)
     return pl.pallas_call(
         functools.partial(momentum_kernel, tile, widths),
         out_shape=pltpu.HBM((rows, columns), jnp.float32),
-        in_specs=[ANY, ANY, ANY] + [VMEM] * len(widths),
+        in_specs=[ANY, ANY, ANY] + [VMEM] * len(widths) + [ANY],
         out_specs=ANY,
         scratch_shapes=[pltpu.VMEM((rank, columns), jnp.bfloat16)],
         compiler_params=pltpu.CompilerParams(vmem_limit_bytes=30 * MIB),
         cost_estimate=cost(10),
         name="new_momentum",
-    )(in_hbm(ortho), *map(in_hbm, halves), *rights)
+    )(in_hbm(ortho), *halves, *rights, in_hbm(before))
 
 
 def weight_kernel(tile, widths, factor, squares, ortho, weight, *refs):
@@ -444,17 +452,13 @@
         place = ((index % 2) * 4 + (index // 2 % 2) * 2 + index // 4 % 2).astype(jnp.int32).reshape(1)
     halves, partials, theirs, projs, sums = None, [], [], [], None
     for i, (start, count) in enumerate(bounds):
-        if i == 3:
-            proj, sums = project(place, 0, partials[:1], theirs[:1], halves, partials[-1], None, widths)
-            projs.append(proj)
-        earlier = (theirs[i - 2 : i - 1] if i > 1 else []) + projs
+        earlier = theirs[i - 2 : i - 1] if i > 1 else []
         halves, (partial,) = partial_products(start, [count], momentum, grad, right_factor, halves, *earlier)
         partials.append(partial)
         theirs.append(swap_pairs(partial, "col", 2, 1) if col_count == 2 else lax.psum(partial, "col") - partial)
-    for i in range(len(projs), len(bounds)):
-        proj, sums = project(
-            place, bounds[i][0], [partials[i]], [theirs[i]], halves, partials[-1], sums, widths
-        )
+    for group in ([0, 1], [2], [3]) if len(bounds) == 4 else [[i] for i in range(len(bounds))]:
+        mine, other = [partials[i] for i in group], [theirs[i] for i in group]
+        proj, sums = project(place, bounds[group[0]][0], mine, other, halves, partials[-1], sums, widths)
         projs.append(proj)
     turned, back = sums_over(sums, "row", row_count, functools.partial(inverse_factor, place))
     ortho = make_ortho(back, jnp.concatenate(projs, axis=0))
@@ -464,10 +468,10 @@
         squares = squares + swap_pairs(squares, "col", 2, 1)
     else:
         squares = lax.psum(squares, "col")
-    new_momentum = make_momentum(ortho, halves, rights, widths)
     whole_rows, whole_columns = rows * row_count, columns * col_count
     factor = step_rate * (whole_rows * whole_columns / rank) ** 0.5
     new_weight = make_weight(factor, squares, weight, ortho, rights, widths)
+    new_momentum = make_momentum(ortho, halves, rights, widths, new_weight)
     share = columns // row_count
     right = jnp.concatenate(rights, axis=1)
     inverse = 1.0 / jnp.sqrt(squares[0] + epsilon)

time: 157 us -> 148 us (0.943)
  Pallas kernels: 97.8 us -> 89.2 us
  waiting for transfers between devices: 22.1 us -> 26.3 us
  local copies, waits for them, and re-layouts: 5.92 us -> 3.06 us
    pallas_call x1, Pallas kernels: 14.9 us -> 8.97 us  [make_momentum(): pl.pallas_call(functools.partial(momentum_kernel, tile, widths), out_shap...]
    ppermute x23, waiting for transfers between devices: 22.1 us -> 26.3 us  [swap_pairs(): return lax.ppermute(x, axis, [(i, i ^ stride) for i in range(count)])]
    pallas_call x4 -> x3, Pallas kernels: 24.6 us -> 20.8 us  [project(): pl.pallas_call(functools.partial(project_kernel, start, widths, step, fir...]
    unnamed x31 -> x25, local copies, waits for them, and re-layouts: 5.75 us -> 2.88 us
  transfers between devices with their start and end apart: 23 -> 23, of which waited for: 8 -> 11; matrix products, arithmetic and copies ran while one was open for 0% -> 0% of each run, Pallas kernels for 44% -> 35%
where the time goes in v1:
time: 148 us
  Pallas kernels  89.2 us (60%)
  starting transfers between devices  27.5 us (19%)
  waiting for transfers between devices  26.3 us (18%)
  local copies, waits for them, and re-layouts  3.06 us (2%)
    ppermute x23, starting transfers between devices, swap_pairs(): return lax.ppermute(x, axis, [(i, i ^ stride) for i in range(count)])  27.5 us
    ppermute x23, waiting for transfers between devices, swap_pairs(): return lax.ppermute(x, axis, [(i, i ^ stride) for i in range(count)])  26.3 us
    pallas_call x4, Pallas kernels, partial_products(): pl.pallas_call(functools.partial(partial_kernel, start, counts, tile), ou...  26 us
    pallas_call x3, Pallas kernels, project(): pl.pallas_call(functools.partial(project_kernel, start, widths, step, fir...  20.8 us
    pallas_call x1, Pallas kernels, make_weight(): pl.pallas_call(functools.partial(weight_kernel, tile, widths, factor), ou...  17.8 us
    pallas_call x1, Pallas kernels, inverse_factor(): pl.pallas_call(functools.partial(inverse_factor_kernel, size, 16, 128), o...  10.7 us
    pallas_call x1, Pallas kernels, make_momentum(): pl.pallas_call(functools.partial(momentum_kernel, tile, widths), out_shap...  8.97 us
  transfers between devices with their start and end apart: 23, of which 11 were waited for; matrix products, arithmetic and copies ran while one was open for 0% of the time, Pallas kernels for 35%

profile of v1, /device:TPU:0, one launch (start us, length us, event | category | flops | bytes accessed | tf_op | source)
XLA Modules:
  0.0 147.7 jit_solution(15461856286698965344)
XLA Ops:
  0.6 4.5 %partial_proj.4 = (bf16[1600,2560]{1,0:T(8,128)(2,1)}, bf16[1600,2560]{1,0:T(8,128)(2,1)}, f32[256,256]{1,0:T(8,128)}) custom-call(f32[1600,2560]{1,0:T(8,128)} %momentum.7, f32[1600,2560]{1,0:T(8,128)} %grad.7, bf16[2560,256]{1,0:T(8,128)(2,1)} %right_factor.7), custom_call_target="tpu_custom_call" | custom-call | flops 2951680000 | tf_op jit(solution)/shard_map/partial_proj/pallas_call | solution.py:86
  5.1 3.0 %collective-permute-start = (f32[256,256]{1,0:T(8,128)}, f32[256,256]{1,0:T(8,128)S(1)}, u32[]{:S(2)}, u32[]{:S(2)}) collective-permute-start(f32[256,256]{1,0:T(8,128)} %get-tuple-element.32.refs_0_), channel_id=1, source_target_pairs={{0,1},{1,0},{2,3},{3,2},{4,5},{5,4},{6,7},{7,6},{8,9},{9,8},{10,11... | collective-permute-start | bytes 786440 | tf_op jit(solution)/shard_map/ppermute | solution.py:359
  8.2 7.8 %partial_proj.5 = (bf16[1600,2560]{1,0:T(8,128)(2,1)}, bf16[1600,2560]{1,0:T(8,128)(2,1)}, f32[512,256]{1,0:T(8,128)}) custom-call(f32[1600,2560]{1,0:T(8,128)} %momentum.7, f32[1600,2560]{1,0:T(8,128)} %grad.7, bf16[2560,256]{1,0:T(8,128)(2,1)} %right_factor.7, ...), custom_call_target="tpu_custom_call", output_to_operand_aliasing={{0}: (3, {}), {1}: (4, {})} | custom-call | flops 5903360000 | tf_op jit(solution)/shard_map/partial_proj/pallas_call | solution.py:86
  16.1 9.1 %partial_proj.6 = (bf16[1600,2560]{1,0:T(8,128)(2,1)}, bf16[1600,2560]{1,0:T(8,128)(2,1)}, f32[576,256]{1,0:T(8,128)}) custom-call(f32[1600,2560]{1,0:T(8,128)} %momentum.7, f32[1600,2560]{1,0:T(8,128)} %grad.7, bf16[2560,256]{1,0:T(8,128)(2,1)} %right_factor.7, ...), custom_call_target="tpu_custom_call", output_to_operand_aliasing={{0}: (3, {}), {1}: (4, {})} | custom-call | flops 6641280000 | tf_op jit(solution)/shard_map/partial_proj/pallas_call | solution.py:86
  25.2 2.0 %collective-permute-start.3 = (f32[576,256]{1,0:T(8,128)}, f32[576,256]{1,0:T(8,128)S(1)}, u32[]{:S(2)}, u32[]{:S(2)}) collective-permute-start(f32[576,256]{1,0:T(8,128)} %get-tuple-element.39.refs_0_), channel_id=1, source_target_pairs={{0,1},{1,0},{2,3},{3,2},{4,5},{5,4},{6,7},{7,6},{8,9},{9,8},{10,11... | collective-permute-start | bytes 1769480 | tf_op jit(solution)/shard_map/ppermute | solution.py:359
  27.2 3.9 %collective-permute-done.1.refs_2_.refs_3_ = f32[512,256]{1,0:T(8,128)S(1)} collective-permute-done((f32[512,256]{1,0:T(8,128)}, f32[512,256]{1,0:T(8,128)S(1)}, u32[]{:S(2)}, u32[]{:S(2)}) %collective-permute-start.1) | collective-permute-done | bytes 524320 | tf_op jit(solution)/shard_map/ppermute | solution.py:359
  31.1 4.6 %partial_proj.7 = (bf16[1600,2560]{1,0:T(8,128)(2,1)}, bf16[1600,2560]{1,0:T(8,128)(2,1)}, f32[256,256]{1,0:T(8,128)}) custom-call(f32[1600,2560]{1,0:T(8,128)} %momentum.7, f32[1600,2560]{1,0:T(8,128)} %grad.7, bf16[2560,256]{1,0:T(8,128)(2,1)} %right_factor.7, ...), custom_call_target="tpu_custom_call", output_to_operand_aliasing={{0}: (3, {}), {1}: (4, {})} | custom-call | flops 2951680000 | tf_op jit(solution)/shard_map/partial_proj/pallas_call | solution.py:86
  36.8 7.9 %turned_product.3 = (f32[768,256]{1,0:T(8,128)S(1)}, f32[256,1280]{1,0:T(8,128)S(1)}, f32[256,1536]{1,0:T(8,128)S(1)}) custom-call(s32[1]{0:T(128)} %bitcast.place, bf16[1600,2560]{1,0:T(8,128)(2,1)} %get-tuple-element.36.high_in, bf16[1600,2560]{1,0:T(8,128)(2,1)} %get-tuple-element.37.low_in, f32[256,256]{1,0:T(8,128)S(1)} %copy-done, ...), custom_call_target="tpu_custom_call" | custom-call | flops 8532199936 | tf_op jit(solution)/shard_map/turned_product/pallas_call | solution.py:152
  44.7 7.6 %turned_product.4 = (f32[576,256]{1,0:T(8,128)S(1)}, f32[256,1280]{1,0:T(8,128)S(1)}, f32[256,1536]{1,0:T(8,128)S(1)}) custom-call(s32[1]{0:T(128)} %bitcast.place, bf16[1600,2560]{1,0:T(8,128)(2,1)} %get-tuple-element.36.high_in, bf16[1600,2560]{1,0:T(8,128)(2,1)} %get-tuple-element.37.low_in, ...), custom_call_target="tpu_custom_call", output_to_operand_aliasing={{1}: (6, {}), {2}: (7, {})} | custom-call | flops 6687399936 | tf_op jit(solution)/shard_map/turned_product/pallas_call | solution.py:152
  52.4 5.3 %turned_product.5 = (f32[256,256]{1,0:T(8,128)S(1)}, f32[256,1280]{1,0:T(8,128)S(1)}, f32[256,1536]{1,0:T(8,128)S(1)}) custom-call(s32[1]{0:T(128)} %bitcast.place, bf16[1600,2560]{1,0:T(8,128)(2,1)} %get-tuple-element.36.high_in, bf16[1600,2560]{1,0:T(8,128)(2,1)} %get-tuple-element.37.low_in, ...), custom_call_target="tpu_custom_call", output_to_operand_aliasing={{1}: (6, {}), {2}: (7, {})} | custom-call | flops 3612733440 | tf_op jit(solution)/shard_map/turned_product/pallas_call | solution.py:152
  58.4 1.5 collective-permute-done.4
  60.0 1.6 %collective-permute-start.7 = (f32[32,1280]{1,0:T(8,128)S(1)}, f32[32,1280]{1,0:T(8,128)S(1)}, u32[]{:S(2)}, u32[]{:S(2)}) collective-permute-start(f32[32,1280]{1,0:T(8,128)S(1)} %get-tuple-element.60), channel_id=1, source_target_pairs={{0,8},{2,10},{4,12},{6,14},{8,0},{10,2},{12,4},{14,6},{16,24},{18,... | collective-permute-start | bytes 491528 | tf_op jit(solution)/shard_map/ppermute | solution.py:359
  61.7 1.4 collective-permute-start.6
  63.8 1.6 %collective-permute-start.12 = (f32[32,1536]{1,0:T(8,128)S(1)}, f32[32,1536]{1,0:T(8,128)S(1)}, u32[]{:S(2)}, u32[]{:S(2)}) collective-permute-start(f32[32,1536]{1,0:T(8,128)S(1)} %get-tuple-element.57), channel_id=1, source_target_pairs={{0,8},{2,10},{4,12},{6,14},{8,0},{10,2},{12,4},{14,6},{16,24},{18,... | collective-permute-start | bytes 589832 | tf_op jit(solution)/shard_map/ppermute | solution.py:359
  65.4 1.4 collective-permute-start.11
  67.1 1.5 %collective-permute-start.10 = (f32[32,1536]{1,0:T(8,128)S(1)}, f32[32,1536]{1,0:T(8,128)S(1)}, u32[]{:S(2)}, u32[]{:S(2)}) collective-permute-start(f32[32,1536]{1,0:T(8,128)S(1)} %get-tuple-element.56), channel_id=1, source_target_pairs={{0,4},{2,6},{4,0},{6,2},{8,12},{10,14},{12,8},{14,10},{16,20},{18,... | collective-permute-start | bytes 589832 | tf_op jit(solution)/shard_map/ppermute | solution.py:359
  68.7 3.0 %collective-permute-done.6 = f32[32,1280]{1,0:T(8,128)S(1)} collective-permute-done((f32[32,1280]{1,0:T(8,128)S(1)}, f32[32,1280]{1,0:T(8,128)S(1)}, u32[]{:S(2)}, u32[]{:S(2)}) %collective-permute-start.6) | collective-permute-done | bytes 163872 | tf_op jit(solution)/shard_map/ppermute | solution.py:359
  71.7 1.9 %collective-permute-done.5 = f32[32,1280]{1,0:T(8,128)S(1)} collective-permute-done((f32[32,1280]{1,0:T(8,128)S(1)}, f32[32,1280]{1,0:T(8,128)S(1)}, u32[]{:S(2)}, u32[]{:S(2)}) %collective-permute-start.5) | collective-permute-done | bytes 163872 | tf_op jit(solution)/shard_map/ppermute | solution.py:359
  73.6 2.7 %collective-permute-start.8 = (f32[32,1280]{1,0:T(8,128)S(1)}, f32[32,1280]{1,0:T(8,128)S(1)}, u32[]{:S(2)}, u32[]{:S(2)}) collective-permute-start(f32[32,1280]{1,0:T(8,128)S(1)} %fusion.6.x), channel_id=1, source_target_pairs={{0,16},{2,18},{4,20},{6,22},{8,24},{10,26},{12,28},{14,30},{16,0},... | collective-permute-start | bytes 491528 | tf_op jit(solution)/shard_map/ppermute | solution.py:359
  76.7 6.1 %collective-permute-done.11 = f32[32,1536]{1,0:T(8,128)S(1)} collective-permute-done((f32[32,1536]{1,0:T(8,128)S(1)}, f32[32,1536]{1,0:T(8,128)S(1)}, u32[]{:S(2)}, u32[]{:S(2)}) %collective-permute-start.11) | collective-permute-done | bytes 196640 | tf_op jit(solution)/shard_map/ppermute | solution.py:359
  83.4 3.1 %collective-permute-start.13 = (f32[32,1280]{1,0:T(8,128)S(1)}, f32[32,1280]{1,0:T(8,128)S(1)}, u32[]{:S(2)}, u32[]{:S(2)}) collective-permute-start(f32[32,1280]{1,0:T(8,128)S(1)} %add_pieces.1.refs_0_), channel_id=1, source_target_pairs={{0,8},{2,10},{4,12},{6,14},{8,0},{10,2},{12,4},{14,6},{16,24},{18,... | collective-permute-start | bytes 491528 | tf_op jit(solution)/shard_map/ppermute | solution.py:359
  86.5 1.5 %collective-permute-start.15 = (f32[32,1280]{1,0:T(8,128)S(1)}, f32[32,1280]{1,0:T(8,128)S(1)}, u32[]{:S(2)}, u32[]{:S(2)}) collective-permute-start(f32[32,1280]{1,0:T(8,128)S(1)} %add_pieces.1.refs_0_), channel_id=1, source_target_pairs={{0,12},{2,14},{4,8},{6,10},{8,4},{10,6},{12,0},{14,2},{16,28},{18,... | collective-permute-start | bytes 491528 | tf_op jit(solution)/shard_map/ppermute | solution.py:359
  88.1 6.2 %collective-permute-done.16 = f32[32,1536]{1,0:T(8,128)S(1)} collective-permute-done((f32[32,1536]{1,0:T(8,128)S(1)}, f32[32,1536]{1,0:T(8,128)S(1)}, u32[]{:S(2)}, u32[]{:S(2)}) %collective-permute-start.16) | collective-permute-done | bytes 196640 | tf_op jit(solution)/shard_map/ppermute | solution.py:359
  94.6 2.4 %collective-permute-done.15.refs_3_ = f32[32,1280]{1,0:T(8,128)S(1)} collective-permute-done((f32[32,1280]{1,0:T(8,128)S(1)}, f32[32,1280]{1,0:T(8,128)S(1)}, u32[]{:S(2)}, u32[]{:S(2)}) %collective-permute-start.15) | collective-permute-done | bytes 163872 | tf_op jit(solution)/shard_map/ppermute | solution.py:359
  97.3 1.6 %collective-permute-start.19 = (f32[32,1536]{1,0:T(8,128)S(1)}, f32[32,1536]{1,0:T(8,128)S(1)}, u32[]{:S(2)}, u32[]{:S(2)}) collective-permute-start(f32[32,1536]{1,0:T(8,128)S(1)} %add.78.refs_4_.before.refs_0_), channel_id=1, source_target_pairs={{0,4},{2,6},{4,0},{6,2},{8,12},{10,14},{12,8},{14,10},{16,20},{18,... | collective-permute-start | bytes 589832 | tf_op jit(solution)/shard_map/ppermute | solution.py:359
  99.0 1.7 %collective-permute-start.20 = (f32[32,1536]{1,0:T(8,128)S(1)}, f32[32,1536]{1,0:T(8,128)S(1)}, u32[]{:S(2)}, u32[]{:S(2)}) collective-permute-start(f32[32,1536]{1,0:T(8,128)S(1)} %add.78.refs_4_.before.refs_0_), channel_id=1, source_target_pairs={{0,12},{2,14},{4,8},{6,10},{8,4},{10,6},{12,0},{14,2},{16,28},{18,... | collective-permute-start | bytes 589832 | tf_op jit(solution)/shard_map/ppermute | solution.py:359
  100.7 10.7 %inverse_factor.1.back.refs_4_ = f32[256,256]{1,0:T(8,128)S(1)} custom-call(s32[1]{0:T(128)} %bitcast.place, f32[128,1280]{1,0:T(8,128)S(1)} %join_pieces.2.own, f32[128,1280]{1,0:T(8,128)S(1)} %collective-permute-done.17.other, f32[32,1536]{1,0:T(8,128)S(1)} %add.78.refs_4_.before.refs_0_), custom_call_target="tpu_custom_call" | custom-call | flops 12682999808 | tf_op jit(solution)/shard_map/inverse_factor/pallas_call | solution.py:212
  113.9 1.0 right_columns.3
  114.9 2.1 %collective-permute-start.22 = (f32[8,256]{1,0:T(8,128)S(1)}, f32[8,256]{1,0:T(8,128)S(1)}, u32[]{:S(2)}, u32[]{:S(2)}) collective-permute-start(f32[8,256]{1,0:T(8,128)S(1)} %add.79), channel_id=1, source_target_pairs={{0,1},{1,0},{2,3},{3,2},{4,5},{5,4},{6,7},{7,6},{8,9},{9,8},{10,11... | collective-permute-start | bytes 24584 | tf_op jit(solution)/shard_map/ppermute | solution.py:359
  116.9 2.9 %ortho.1 = f32[1600,256]{1,0:T(8,128)} custom-call(f32[256,256]{1,0:T(8,128)S(1)} %inverse_factor.1.back.refs_4_, f32[1600,256]{1,0:T(8,128)S(1)} %pad_maximum_fusion.proj), custom_call_target="tpu_custom_call" | custom-call | flops 2305999872 | tf_op jit(solution)/shard_map/ortho/pallas_call | solution.py:265
  119.9 17.8 %new_weight.1.refs_2_ = f32[1600,2560]{1,0:T(8,128)} custom-call(f32[8,256]{1,0:T(8,128)S(1)} %add.80.squares, f32[1600,256]{1,0:T(8,128)} %ortho.1, f32[1600,2560]{1,0:T(8,128)} %weight.1, f32[256,1024]{1,0:T(8,128)S(1)} %get-tuple-element.51.refs_0_, f32[256,1536]{1,0:T(8,128)S(1)} %get-tuple-element.52.refs_1_), custom_call_target="tpu_custom_call" | custom-call | flops 11530000384 | tf_op jit(solution)/shard_map/new_weight/pallas_call | solution.py:346
  137.8 9.0 %new_momentum.1 = f32[1600,2560]{1,0:T(8,128)} custom-call(f32[1600,256]{1,0:T(8,128)} %ortho.1, bf16[1600,2560]{1,0:T(8,128)(2,1)S(1)} %bitcast.5, bf16[1600,2560]{1,0:T(8,128)(2,1)S(1)} %bitcast.7, f32[256,1024]{1,0:T(8,128)S(1)} %get-tuple-element.51.refs_0_, f32[256,1536]{1,0:T(8,128)S(1)} %get-tuple-element.52.refs_1_, f32[1600,2560]{1,0:T(8,128)} %new_weight.1.refs_2_), custom_call_target="tpu_custom_call" | custom-call | flops 11530000384 | tf_op jit(solution)/shard_map/new_momentum/pallas_call | solution.py:304
  (71 shorter events, 8.1 us)
Async XLA Ops:
  5.1 11.0 %collective-permute-start = (f32[256,256]{1,0:T(8,128)}, f32[256,256]{1,0:T(8,128)S(1)}, u32[]{:S(2)}, u32[]{:S(2)}) collective-permute-start(f32[256,256]{1,0:T(8,128)} %get-tuple-element.32.refs_0_), channel_id=1, source_target_pairs={{0,1},{1,0},{2,3},{3,2},{4,5},{5,4},{6,7},{7,6},{8,9},{9,8},{10,11... | collective-permute-start | bytes 786440 | tf_op jit(solution)/shard_map/ppermute | solution.py:359
  16.0 15.1 %collective-permute-start.1 = (f32[512,256]{1,0:T(8,128)}, f32[512,256]{1,0:T(8,128)S(1)}, u32[]{:S(2)}, u32[]{:S(2)}) collective-permute-start(f32[512,256]{1,0:T(8,128)} %get-tuple-element.35.refs_1_), channel_id=1, source_target_pairs={{0,1},{1,0},{2,3},{3,2},{4,5},{5,4},{6,7},{7,6},{8,9},{9,8},{10,11... | collective-permute-start | bytes 1572872 | tf_op jit(solution)/shard_map/ppermute | solution.py:359
  25.2 19.5 %collective-permute-start.3 = (f32[576,256]{1,0:T(8,128)}, f32[576,256]{1,0:T(8,128)S(1)}, u32[]{:S(2)}, u32[]{:S(2)}) collective-permute-start(f32[576,256]{1,0:T(8,128)} %get-tuple-element.39.refs_0_), channel_id=1, source_target_pairs={{0,1},{1,0},{2,3},{3,2},{4,5},{5,4},{6,7},{7,6},{8,9},{9,8},{10,11... | collective-permute-start | bytes 1769480 | tf_op jit(solution)/shard_map/ppermute | solution.py:359
  31.1 4.7 %copy-start.6 = (f32[512,256]{1,0:T(8,128)S(1)}, f32[512,256]{1,0:T(8,128)}, u32[]{:S(2)}) copy-start(f32[512,256]{1,0:T(8,128)} %get-tuple-element.35.refs_1_) | copy-start | bytes 1572868
  31.1 4.7 %copy-start.7 = (f32[256,256]{1,0:T(8,128)S(1)}, f32[256,256]{1,0:T(8,128)}, u32[]{:S(2)}) copy-start(f32[256,256]{1,0:T(8,128)} %get-tuple-element.32.refs_0_) | copy-start | bytes 786436
  35.7 16.6 %collective-permute-start.2 = (f32[256,256]{1,0:T(8,128)}, f32[256,256]{1,0:T(8,128)S(1)}, u32[]{:S(2)}, u32[]{:S(2)}) collective-permute-start(f32[256,256]{1,0:T(8,128)} %get-tuple-element.38.before.refs_0_), channel_id=1, source_target_pairs={{0,1},{1,0},{2,3},{3,2},{4,5},{5,4},{6,7},{7,6},{8,9},{9,8},{10,11... | collective-permute-start | bytes 786440 | tf_op jit(solution)/shard_map/ppermute | solution.py:359
  36.8 7.9 %copy-start.5 = (f32[576,256]{1,0:T(8,128)S(1)}, f32[576,256]{1,0:T(8,128)}, u32[]{:S(2)}) copy-start(f32[576,256]{1,0:T(8,128)} %get-tuple-element.39.refs_0_) | copy-start | bytes 1769476
  57.7 2.2 %collective-permute-start.4 = (f32[128,1280]{1,0:T(8,128)S(1)}, f32[128,1280]{1,0:T(8,128)S(1)}, u32[]{:S(2)}, u32[]{:S(2)}) collective-permute-start(f32[128,1280]{1,0:T(8,128)S(1)} %slice.40), channel_id=1, source_target_pairs={{0,2},{2,0},{4,6},{6,4},{8,10},{10,8},{12,14},{14,12},{16,18},{18,... | collective-permute-start | bytes 1966088 | tf_op jit(solution)/shard_map/ppermute | solution.py:359
  57.9 5.7 %collective-permute-start.9 = (f32[128,1536]{1,0:T(8,128)S(1)}, f32[128,1536]{1,0:T(8,128)S(1)}, u32[]{:S(2)}, u32[]{:S(2)}) collective-permute-start(f32[128,1536]{1,0:T(8,128)S(1)} %slice.46), channel_id=1, source_target_pairs={{0,2},{2,0},{4,6},{6,4},{8,10},{10,8},{12,14},{14,12},{16,18},{18,... | collective-permute-start | bytes 2359304 | tf_op jit(solution)/shard_map/ppermute | solution.py:359
  60.0 7.1 %collective-permute-start.7 = (f32[32,1280]{1,0:T(8,128)S(1)}, f32[32,1280]{1,0:T(8,128)S(1)}, u32[]{:S(2)}, u32[]{:S(2)}) collective-permute-start(f32[32,1280]{1,0:T(8,128)S(1)} %get-tuple-element.60), channel_id=1, source_target_pairs={{0,8},{2,10},{4,12},{6,14},{8,0},{10,2},{12,4},{14,6},{16,24},{18,... | collective-permute-start | bytes 491528 | tf_op jit(solution)/shard_map/ppermute | solution.py:359
  61.7 10.0 %collective-permute-start.6 = (f32[32,1280]{1,0:T(8,128)S(1)}, f32[32,1280]{1,0:T(8,128)S(1)}, u32[]{:S(2)}, u32[]{:S(2)}) collective-permute-start(f32[32,1280]{1,0:T(8,128)S(1)} %get-tuple-element.61), channel_id=1, source_target_pairs={{0,12},{2,14},{4,8},{6,10},{8,4},{10,6},{12,0},{14,2},{16,28},{18,... | collective-permute-start | bytes 491528 | tf_op jit(solution)/shard_map/ppermute | solution.py:359
  63.1 10.5 %collective-permute-start.5 = (f32[32,1280]{1,0:T(8,128)S(1)}, f32[32,1280]{1,0:T(8,128)S(1)}, u32[]{:S(2)}, u32[]{:S(2)}) collective-permute-start(f32[32,1280]{1,0:T(8,128)S(1)} %get-tuple-element.59), channel_id=1, source_target_pairs={{0,4},{2,6},{4,0},{6,2},{8,12},{10,14},{12,8},{14,10},{16,20},{18,... | collective-permute-start | bytes 491528 | tf_op jit(solution)/shard_map/ppermute | solution.py:359
  63.8 12.9 %collective-permute-start.12 = (f32[32,1536]{1,0:T(8,128)S(1)}, f32[32,1536]{1,0:T(8,128)S(1)}, u32[]{:S(2)}, u32[]{:S(2)}) collective-permute-start(f32[32,1536]{1,0:T(8,128)S(1)} %get-tuple-element.57), channel_id=1, source_target_pairs={{0,8},{2,10},{4,12},{6,14},{8,0},{10,2},{12,4},{14,6},{16,24},{18,... | collective-permute-start | bytes 589832 | tf_op jit(solution)/shard_map/ppermute | solution.py:359
  65.4 17.4 %collective-permute-start.11 = (f32[32,1536]{1,0:T(8,128)S(1)}, f32[32,1536]{1,0:T(8,128)S(1)}, u32[]{:S(2)}, u32[]{:S(2)}) collective-permute-start(f32[32,1536]{1,0:T(8,128)S(1)} %get-tuple-element.58), channel_id=1, source_target_pairs={{0,12},{2,14},{4,8},{6,10},{8,4},{10,6},{12,0},{14,2},{16,28},{18,... | collective-permute-start | bytes 589832 | tf_op jit(solution)/shard_map/ppermute | solution.py:359
  67.1 15.7 %collective-permute-start.10 = (f32[32,1536]{1,0:T(8,128)S(1)}, f32[32,1536]{1,0:T(8,128)S(1)}, u32[]{:S(2)}, u32[]{:S(2)}) collective-permute-start(f32[32,1536]{1,0:T(8,128)S(1)} %get-tuple-element.56), channel_id=1, source_target_pairs={{0,4},{2,6},{4,0},{6,2},{8,12},{10,14},{12,8},{14,10},{16,20},{18,... | collective-permute-start | bytes 589832 | tf_op jit(solution)/shard_map/ppermute | solution.py:359
  73.6 9.8 %collective-permute-start.8 = (f32[32,1280]{1,0:T(8,128)S(1)}, f32[32,1280]{1,0:T(8,128)S(1)}, u32[]{:S(2)}, u32[]{:S(2)}) collective-permute-start(f32[32,1280]{1,0:T(8,128)S(1)} %fusion.6.x), channel_id=1, source_target_pairs={{0,16},{2,18},{4,20},{6,22},{8,24},{10,26},{12,28},{14,30},{16,0},... | collective-permute-start | bytes 491528 | tf_op jit(solution)/shard_map/ppermute | solution.py:359
  82.9 11.4 %collective-permute-start.16 = (f32[32,1536]{1,0:T(8,128)S(1)}, f32[32,1536]{1,0:T(8,128)S(1)}, u32[]{:S(2)}, u32[]{:S(2)}) collective-permute-start(f32[32,1536]{1,0:T(8,128)S(1)} %fusion.4.before), channel_id=1, source_target_pairs={{0,16},{2,18},{4,20},{6,22},{8,24},{10,26},{12,28},{14,30},{16,0},... | collective-permute-start | bytes 589832 | tf_op jit(solution)/shard_map/ppermute | solution.py:359
  83.4 11.2 %collective-permute-start.13 = (f32[32,1280]{1,0:T(8,128)S(1)}, f32[32,1280]{1,0:T(8,128)S(1)}, u32[]{:S(2)}, u32[]{:S(2)}) collective-permute-start(f32[32,1280]{1,0:T(8,128)S(1)} %add_pieces.1.refs_0_), channel_id=1, source_target_pairs={{0,8},{2,10},{4,12},{6,14},{8,0},{10,2},{12,4},{14,6},{16,24},{18,... | collective-permute-start | bytes 491528 | tf_op jit(solution)/shard_map/ppermute | solution.py:359
  86.5 8.1 %collective-permute-start.14 = (f32[32,1280]{1,0:T(8,128)S(1)}, f32[32,1280]{1,0:T(8,128)S(1)}, u32[]{:S(2)}, u32[]{:S(2)}) collective-permute-start(f32[32,1280]{1,0:T(8,128)S(1)} %add_pieces.1.refs_0_), channel_id=1, source_target_pairs={{0,4},{2,6},{4,0},{6,2},{8,12},{10,14},{12,8},{14,10},{16,20},{18,... | collective-permute-start | bytes 491528 | tf_op jit(solution)/shard_map/ppermute | solution.py:359
  86.5 10.5 %collective-permute-start.15 = (f32[32,1280]{1,0:T(8,128)S(1)}, f32[32,1280]{1,0:T(8,128)S(1)}, u32[]{:S(2)}, u32[]{:S(2)}) collective-permute-start(f32[32,1280]{1,0:T(8,128)S(1)} %add_pieces.1.refs_0_), channel_id=1, source_target_pairs={{0,12},{2,14},{4,8},{6,10},{8,4},{10,6},{12,0},{14,2},{16,28},{18,... | collective-permute-start | bytes 491528 | tf_op jit(solution)/shard_map/ppermute | solution.py:359
  97.0 14.4 %copy-start.1 = (f32[128,1280]{1,0:T(8,128)}, f32[128,1280]{1,0:T(8,128)S(1)}, u32[]{:S(2)}) copy-start(f32[128,1280]{1,0:T(8,128)S(1)} %join_pieces.2.own) | copy-start | bytes 1966084
  97.1 3.6 %collective-permute-start.17 = (f32[128,1280]{1,0:T(8,128)S(1)}, f32[128,1280]{1,0:T(8,128)S(1)}, u32[]{:S(2)}, u32[]{:S(2)}) collective-permute-start(f32[128,1280]{1,0:T(8,128)S(1)} %join_pieces.2.own), channel_id=1, source_target_pairs={{0,2},{2,0},{4,6},{6,4},{8,10},{10,8},{12,14},{14,12},{16,18},{18,... | collective-permute-start | bytes 1966088 | tf_op jit(solution)/shard_map/ppermute | solution.py:359
  97.1 14.3 %collective-permute-start.18 = (f32[32,1536]{1,0:T(8,128)S(1)}, f32[32,1536]{1,0:T(8,128)S(1)}, u32[]{:S(2)}, u32[]{:S(2)}) collective-permute-start(f32[32,1536]{1,0:T(8,128)S(1)} %add.78.refs_4_.before.refs_0_), channel_id=1, source_target_pairs={{0,8},{2,10},{4,12},{6,14},{8,0},{10,2},{12,4},{14,6},{16,24},{18,... | collective-permute-start | bytes 589832 | tf_op jit(solution)/shard_map/ppermute | solution.py:359
  97.3 14.1 %collective-permute-start.19 = (f32[32,1536]{1,0:T(8,128)S(1)}, f32[32,1536]{1,0:T(8,128)S(1)}, u32[]{:S(2)}, u32[]{:S(2)}) collective-permute-start(f32[32,1536]{1,0:T(8,128)S(1)} %add.78.refs_4_.before.refs_0_), channel_id=1, source_target_pairs={{0,4},{2,6},{4,0},{6,2},{8,12},{10,14},{12,8},{14,10},{16,20},{18,... | collective-permute-start | bytes 589832 | tf_op jit(solution)/shard_map/ppermute | solution.py:359
  99.0 12.5 %collective-permute-start.20 = (f32[32,1536]{1,0:T(8,128)S(1)}, f32[32,1536]{1,0:T(8,128)S(1)}, u32[]{:S(2)}, u32[]{:S(2)}) collective-permute-start(f32[32,1536]{1,0:T(8,128)S(1)} %add.78.refs_4_.before.refs_0_), channel_id=1, source_target_pairs={{0,12},{2,14},{4,8},{6,10},{8,4},{10,6},{12,0},{14,2},{16,28},{18,... | collective-permute-start | bytes 589832 | tf_op jit(solution)/shard_map/ppermute | solution.py:359
  100.7 10.7 %copy-start.3 = (f32[128,1280]{1,0:T(8,128)}, f32[128,1280]{1,0:T(8,128)S(1)}, u32[]{:S(2)}) copy-start(f32[128,1280]{1,0:T(8,128)S(1)} %collective-permute-done.17.other) | copy-start | bytes 1966084
  111.5 2.4 %collective-permute-start.21 = (f32[128,1536]{1,0:T(8,128)S(1)}, f32[128,1536]{1,0:T(8,128)S(1)}, u32[]{:S(2)}, u32[]{:S(2)}) collective-permute-start(f32[128,1536]{1,0:T(8,128)S(1)} %join_pieces.3.own), channel_id=1, source_target_pairs={{0,2},{2,0},{4,6},{6,4},{8,10},{10,8},{12,14},{14,12},{16,18},{18,... | collective-permute-start | bytes 2359304 | tf_op jit(solution)/shard_map/ppermute | solution.py:359
  114.9 5.0 %collective-permute-start.22 = (f32[8,256]{1,0:T(8,128)S(1)}, f32[8,256]{1,0:T(8,128)S(1)}, u32[]{:S(2)}, u32[]{:S(2)}) collective-permute-start(f32[8,256]{1,0:T(8,128)S(1)} %add.79), channel_id=1, source_target_pairs={{0,1},{1,0},{2,3},{3,2},{4,5},{5,4},{6,7},{7,6},{8,9},{9,8},{10,11... | collective-permute-start | bytes 24584 | tf_op jit(solution)/shard_map/ppermute | solution.py:359
  116.9 20.8 %slice-start = ((s8[8192000]{0:T(1024)(128)(4,1)}), s8[4194304]{0:T(1024)(128)(4,1)S(1)}, s32[]{:S(2)}) async-start(s8[8192000]{0:T(1024)(128)(4,1)} %bitcast.4), calls=%async_computation | async-start | bytes 8388608
  116.9 20.8 %slice-start.2 = ((s8[8192000]{0:T(1024)(128)(4,1)}), s8[4194304]{0:T(1024)(128)(4,1)S(1)}, s32[]{:S(2)}) async-start(s8[8192000]{0:T(1024)(128)(4,1)} %bitcast.6), calls=%async_computation.2 | async-start | bytes 8388608
  119.9 17.9 %slice-start.1 = ((s8[8192000]{0:T(1024)(128)(4,1)}), s8[3997696]{0:T(1024)(128)(4,1)S(1)}, s32[]{:S(2)}) async-start(s8[8192000]{0:T(1024)(128)(4,1)} %bitcast.4), calls=%async_computation.1 | async-start | bytes 7995392
  119.9 17.9 %slice-start.3 = ((s8[8192000]{0:T(1024)(128)(4,1)}), s8[3997696]{0:T(1024)(128)(4,1)S(1)}, s32[]{:S(2)}) async-start(s8[8192000]{0:T(1024)(128)(4,1)} %bitcast.6), calls=%async_computation.3 | async-start | bytes 7995392
  (3 other events, 3.3 us)

commit v2 on v1

--- a/solution.py
+++ b/solution.py
@@ -210,7 +210,7 @@
 def inverse_factor(place, own, other, before):
     size = 2 * own.shape[0]
     return pl.pallas_call(
-        functools.partial(inverse_factor_kernel, size, 16, 128),
+        functools.partial(inverse_factor_kernel, size, 32, 128),
         out_shape=jax.ShapeDtypeStruct((size, size), jnp.float32),
         in_specs=[SMEM, VMEM, VMEM, ANY],
         out_specs=VMEM,

time: 148 us -> 147 us (level)
  transfers between devices with their start and end apart: 23 -> 23, of which waited for: 11 -> 11; matrix products, arithmetic and copies ran while one was open for 0% -> 0% of each run, Pallas kernels for 35% -> 34%
where the time goes in v2:
time: 147 us
  Pallas kernels  88 us (60%)
  starting transfers between devices  27.5 us (19%)
  waiting for transfers between devices  26.3 us (18%)
  local copies, waits for them, and re-layouts  3.06 us (2%)
    ppermute x23, starting transfers between devices, swap_pairs(): return lax.ppermute(x, axis, [(i, i ^ stride) for i in range(count)])  27.5 us
    ppermute x23, waiting for transfers between devices, swap_pairs(): return lax.ppermute(x, axis, [(i, i ^ stride) for i in range(count)])  26.3 us
    pallas_call x4, Pallas kernels, partial_products(): pl.pallas_call(functools.partial(partial_kernel, start, counts, tile), ou...  26 us
    pallas_call x3, Pallas kernels, project(): pl.pallas_call(functools.partial(project_kernel, start, widths, step, fir...  20.8 us
    pallas_call x1, Pallas kernels, make_weight(): pl.pallas_call(functools.partial(weight_kernel, tile, widths, factor), ou...  17.9 us
    pallas_call x1, Pallas kernels, inverse_factor(): pl.pallas_call(functools.partial(inverse_factor_kernel, size, 32, 128), o...  9.54 us
    pallas_call x1, Pallas kernels, make_momentum(): pl.pallas_call(functools.partial(momentum_kernel, tile, widths), out_shap...  8.97 us
  transfers between devices with their start and end apart: 23, of which 11 were waited for; matrix products, arithmetic and copies ran while one was open for 0% of the time, Pallas kernels for 34%

profile of v2, /device:TPU:0, one launch (start us, length us, event | category | flops | bytes accessed | tf_op | source)
XLA Modules:
  0.0 146.6 jit_solution(4492503585420392926)
XLA Ops:
  0.6 4.5 %partial_proj.4 = (bf16[1600,2560]{1,0:T(8,128)(2,1)}, bf16[1600,2560]{1,0:T(8,128)(2,1)}, f32[256,256]{1,0:T(8,128)}) custom-call(f32[1600,2560]{1,0:T(8,128)} %momentum.7, f32[1600,2560]{1,0:T(8,128)} %grad.7, bf16[2560,256]{1,0:T(8,128)(2,1)} %right_factor.7), custom_call_target="tpu_custom_call" | custom-call | flops 2951680000 | tf_op jit(solution)/shard_map/partial_proj/pallas_call | solution.py:86
  5.1 3.0 %collective-permute-start = (f32[256,256]{1,0:T(8,128)}, f32[256,256]{1,0:T(8,128)S(1)}, u32[]{:S(2)}, u32[]{:S(2)}) collective-permute-start(f32[256,256]{1,0:T(8,128)} %get-tuple-element.32.refs_0_), channel_id=1, source_target_pairs={{0,1},{1,0},{2,3},{3,2},{4,5},{5,4},{6,7},{7,6},{8,9},{9,8},{10,11... | collective-permute-start | bytes 786440 | tf_op jit(solution)/shard_map/ppermute | solution.py:359
  8.2 7.8 %partial_proj.5 = (bf16[1600,2560]{1,0:T(8,128)(2,1)}, bf16[1600,2560]{1,0:T(8,128)(2,1)}, f32[512,256]{1,0:T(8,128)}) custom-call(f32[1600,2560]{1,0:T(8,128)} %momentum.7, f32[1600,2560]{1,0:T(8,128)} %grad.7, bf16[2560,256]{1,0:T(8,128)(2,1)} %right_factor.7, ...), custom_call_target="tpu_custom_call", output_to_operand_aliasing={{0}: (3, {}), {1}: (4, {})} | custom-call | flops 5903360000 | tf_op jit(solution)/shard_map/partial_proj/pallas_call | solution.py:86
  16.1 9.1 %partial_proj.6 = (bf16[1600,2560]{1,0:T(8,128)(2,1)}, bf16[1600,2560]{1,0:T(8,128)(2,1)}, f32[576,256]{1,0:T(8,128)}) custom-call(f32[1600,2560]{1,0:T(8,128)} %momentum.7, f32[1600,2560]{1,0:T(8,128)} %grad.7, bf16[2560,256]{1,0:T(8,128)(2,1)} %right_factor.7, ...), custom_call_target="tpu_custom_call", output_to_operand_aliasing={{0}: (3, {}), {1}: (4, {})} | custom-call | flops 6641280000 | tf_op jit(solution)/shard_map/partial_proj/pallas_call | solution.py:86
  25.2 2.0 %collective-permute-start.3 = (f32[576,256]{1,0:T(8,128)}, f32[576,256]{1,0:T(8,128)S(1)}, u32[]{:S(2)}, u32[]{:S(2)}) collective-permute-start(f32[576,256]{1,0:T(8,128)} %get-tuple-element.39.refs_0_), channel_id=1, source_target_pairs={{0,1},{1,0},{2,3},{3,2},{4,5},{5,4},{6,7},{7,6},{8,9},{9,8},{10,11... | collective-permute-start | bytes 1769480 | tf_op jit(solution)/shard_map/ppermute | solution.py:359
  27.2 3.9 %collective-permute-done.1.refs_2_.refs_3_ = f32[512,256]{1,0:T(8,128)S(1)} collective-permute-done((f32[512,256]{1,0:T(8,128)}, f32[512,256]{1,0:T(8,128)S(1)}, u32[]{:S(2)}, u32[]{:S(2)}) %collective-permute-start.1) | collective-permute-done | bytes 524320 | tf_op jit(solution)/shard_map/ppermute | solution.py:359
  31.1 4.6 %partial_proj.7 = (bf16[1600,2560]{1,0:T(8,128)(2,1)}, bf16[1600,2560]{1,0:T(8,128)(2,1)}, f32[256,256]{1,0:T(8,128)}) custom-call(f32[1600,2560]{1,0:T(8,128)} %momentum.7, f32[1600,2560]{1,0:T(8,128)} %grad.7, bf16[2560,256]{1,0:T(8,128)(2,1)} %right_factor.7, ...), custom_call_target="tpu_custom_call", output_to_operand_aliasing={{0}: (3, {}), {1}: (4, {})} | custom-call | flops 2951680000 | tf_op jit(solution)/shard_map/partial_proj/pallas_call | solution.py:86
  36.8 7.9 %turned_product.3 = (f32[768,256]{1,0:T(8,128)S(1)}, f32[256,1280]{1,0:T(8,128)S(1)}, f32[256,1536]{1,0:T(8,128)S(1)}) custom-call(s32[1]{0:T(128)} %bitcast.place, bf16[1600,2560]{1,0:T(8,128)(2,1)} %get-tuple-element.36.high_in, bf16[1600,2560]{1,0:T(8,128)(2,1)} %get-tuple-element.37.low_in, f32[256,256]{1,0:T(8,128)S(1)} %copy-done, ...), custom_call_target="tpu_custom_call" | custom-call | flops 8532199936 | tf_op jit(solution)/shard_map/turned_product/pallas_call | solution.py:152
  44.7 7.6 %turned_product.4 = (f32[576,256]{1,0:T(8,128)S(1)}, f32[256,1280]{1,0:T(8,128)S(1)}, f32[256,1536]{1,0:T(8,128)S(1)}) custom-call(s32[1]{0:T(128)} %bitcast.place, bf16[1600,2560]{1,0:T(8,128)(2,1)} %get-tuple-element.36.high_in, bf16[1600,2560]{1,0:T(8,128)(2,1)} %get-tuple-element.37.low_in, ...), custom_call_target="tpu_custom_call", output_to_operand_aliasing={{1}: (6, {}), {2}: (7, {})} | custom-call | flops 6687399936 | tf_op jit(solution)/shard_map/turned_product/pallas_call | solution.py:152
  52.4 5.3 %turned_product.5 = (f32[256,256]{1,0:T(8,128)S(1)}, f32[256,1280]{1,0:T(8,128)S(1)}, f32[256,1536]{1,0:T(8,128)S(1)}) custom-call(s32[1]{0:T(128)} %bitcast.place, bf16[1600,2560]{1,0:T(8,128)(2,1)} %get-tuple-element.36.high_in, bf16[1600,2560]{1,0:T(8,128)(2,1)} %get-tuple-element.37.low_in, ...), custom_call_target="tpu_custom_call", output_to_operand_aliasing={{1}: (6, {}), {2}: (7, {})} | custom-call | flops 3612733440 | tf_op jit(solution)/shard_map/turned_product/pallas_call | solution.py:152
  58.4 1.5 collective-permute-done.4
  60.0 1.6 %collective-permute-start.7 = (f32[32,1280]{1,0:T(8,128)S(1)}, f32[32,1280]{1,0:T(8,128)S(1)}, u32[]{:S(2)}, u32[]{:S(2)}) collective-permute-start(f32[32,1280]{1,0:T(8,128)S(1)} %get-tuple-element.60), channel_id=1, source_target_pairs={{0,8},{2,10},{4,12},{6,14},{8,0},{10,2},{12,4},{14,6},{16,24},{18,... | collective-permute-start | bytes 491528 | tf_op jit(solution)/shard_map/ppermute | solution.py:359
  61.7 1.4 collective-permute-start.6
  63.8 1.6 %collective-permute-start.12 = (f32[32,1536]{1,0:T(8,128)S(1)}, f32[32,1536]{1,0:T(8,128)S(1)}, u32[]{:S(2)}, u32[]{:S(2)}) collective-permute-start(f32[32,1536]{1,0:T(8,128)S(1)} %get-tuple-element.57), channel_id=1, source_target_pairs={{0,8},{2,10},{4,12},{6,14},{8,0},{10,2},{12,4},{14,6},{16,24},{18,... | collective-permute-start | bytes 589832 | tf_op jit(solution)/shard_map/ppermute | solution.py:359
  65.4 1.4 collective-permute-start.11
  67.1 1.5 %collective-permute-start.10 = (f32[32,1536]{1,0:T(8,128)S(1)}, f32[32,1536]{1,0:T(8,128)S(1)}, u32[]{:S(2)}, u32[]{:S(2)}) collective-permute-start(f32[32,1536]{1,0:T(8,128)S(1)} %get-tuple-element.56), channel_id=1, source_target_pairs={{0,4},{2,6},{4,0},{6,2},{8,12},{10,14},{12,8},{14,10},{16,20},{18,... | collective-permute-start | bytes 589832 | tf_op jit(solution)/shard_map/ppermute | solution.py:359
  68.7 3.0 %collective-permute-done.6 = f32[32,1280]{1,0:T(8,128)S(1)} collective-permute-done((f32[32,1280]{1,0:T(8,128)S(1)}, f32[32,1280]{1,0:T(8,128)S(1)}, u32[]{:S(2)}, u32[]{:S(2)}) %collective-permute-start.6) | collective-permute-done | bytes 163872 | tf_op jit(solution)/shard_map/ppermute | solution.py:359
  71.7 1.9 %collective-permute-done.5 = f32[32,1280]{1,0:T(8,128)S(1)} collective-permute-done((f32[32,1280]{1,0:T(8,128)S(1)}, f32[32,1280]{1,0:T(8,128)S(1)}, u32[]{:S(2)}, u32[]{:S(2)}) %collective-permute-start.5) | collective-permute-done | bytes 163872 | tf_op jit(solution)/shard_map/ppermute | solution.py:359
  73.6 2.7 %collective-permute-start.8 = (f32[32,1280]{1,0:T(8,128)S(1)}, f32[32,1280]{1,0:T(8,128)S(1)}, u32[]{:S(2)}, u32[]{:S(2)}) collective-permute-start(f32[32,1280]{1,0:T(8,128)S(1)} %fusion.6.x), channel_id=1, source_target_pairs={{0,16},{2,18},{4,20},{6,22},{8,24},{10,26},{12,28},{14,30},{16,0},... | collective-permute-start | bytes 491528 | tf_op jit(solution)/shard_map/ppermute | solution.py:359
  76.7 6.1 %collective-permute-done.11 = f32[32,1536]{1,0:T(8,128)S(1)} collective-permute-done((f32[32,1536]{1,0:T(8,128)S(1)}, f32[32,1536]{1,0:T(8,128)S(1)}, u32[]{:S(2)}, u32[]{:S(2)}) %collective-permute-start.11) | collective-permute-done | bytes 196640 | tf_op jit(solution)/shard_map/ppermute | solution.py:359
  83.4 3.1 %collective-permute-start.13 = (f32[32,1280]{1,0:T(8,128)S(1)}, f32[32,1280]{1,0:T(8,128)S(1)}, u32[]{:S(2)}, u32[]{:S(2)}) collective-permute-start(f32[32,1280]{1,0:T(8,128)S(1)} %add_pieces.1.refs_0_), channel_id=1, source_target_pairs={{0,8},{2,10},{4,12},{6,14},{8,0},{10,2},{12,4},{14,6},{16,24},{18,... | collective-permute-start | bytes 491528 | tf_op jit(solution)/shard_map/ppermute | solution.py:359
  86.5 1.5 %collective-permute-start.15 = (f32[32,1280]{1,0:T(8,128)S(1)}, f32[32,1280]{1,0:T(8,128)S(1)}, u32[]{:S(2)}, u32[]{:S(2)}) collective-permute-start(f32[32,1280]{1,0:T(8,128)S(1)} %add_pieces.1.refs_0_), channel_id=1, source_target_pairs={{0,12},{2,14},{4,8},{6,10},{8,4},{10,6},{12,0},{14,2},{16,28},{18,... | collective-permute-start | bytes 491528 | tf_op jit(solution)/shard_map/ppermute | solution.py:359
  88.1 6.2 %collective-permute-done.16 = f32[32,1536]{1,0:T(8,128)S(1)} collective-permute-done((f32[32,1536]{1,0:T(8,128)S(1)}, f32[32,1536]{1,0:T(8,128)S(1)}, u32[]{:S(2)}, u32[]{:S(2)}) %collective-permute-start.16) | collective-permute-done | bytes 196640 | tf_op jit(solution)/shard_map/ppermute | solution.py:359
  94.6 2.4 %collective-permute-done.15.refs_3_ = f32[32,1280]{1,0:T(8,128)S(1)} collective-permute-done((f32[32,1280]{1,0:T(8,128)S(1)}, f32[32,1280]{1,0:T(8,128)S(1)}, u32[]{:S(2)}, u32[]{:S(2)}) %collective-permute-start.15) | collective-permute-done | bytes 163872 | tf_op jit(solution)/shard_map/ppermute | solution.py:359
  97.3 1.6 %collective-permute-start.19 = (f32[32,1536]{1,0:T(8,128)S(1)}, f32[32,1536]{1,0:T(8,128)S(1)}, u32[]{:S(2)}, u32[]{:S(2)}) collective-permute-start(f32[32,1536]{1,0:T(8,128)S(1)} %add.78.refs_4_.before.refs_0_), channel_id=1, source_target_pairs={{0,4},{2,6},{4,0},{6,2},{8,12},{10,14},{12,8},{14,10},{16,20},{18,... | collective-permute-start | bytes 589832 | tf_op jit(solution)/shard_map/ppermute | solution.py:359
  99.0 1.7 %collective-permute-start.20 = (f32[32,1536]{1,0:T(8,128)S(1)}, f32[32,1536]{1,0:T(8,128)S(1)}, u32[]{:S(2)}, u32[]{:S(2)}) collective-permute-start(f32[32,1536]{1,0:T(8,128)S(1)} %add.78.refs_4_.before.refs_0_), channel_id=1, source_target_pairs={{0,12},{2,14},{4,8},{6,10},{8,4},{10,6},{12,0},{14,2},{16,28},{18,... | collective-permute-start | bytes 589832 | tf_op jit(solution)/shard_map/ppermute | solution.py:359
  100.7 9.5 %inverse_factor.1.back.refs_4_ = f32[256,256]{1,0:T(8,128)S(1)} custom-call(s32[1]{0:T(128)} %bitcast.place, f32[128,1280]{1,0:T(8,128)S(1)} %join_pieces.2.own, f32[128,1280]{1,0:T(8,128)S(1)} %collective-permute-done.17.other, f32[32,1536]{1,0:T(8,128)S(1)} %add.78.refs_4_.before.refs_0_), custom_call_target="tpu_custom_call" | custom-call | flops 12682999808 | tf_op jit(solution)/shard_map/inverse_factor/pallas_call | solution.py:212
  112.7 1.0 right_columns.3
  113.7 2.1 %collective-permute-start.22 = (f32[8,256]{1,0:T(8,128)S(1)}, f32[8,256]{1,0:T(8,128)S(1)}, u32[]{:S(2)}, u32[]{:S(2)}) collective-permute-start(f32[8,256]{1,0:T(8,128)S(1)} %add.79), channel_id=1, source_target_pairs={{0,1},{1,0},{2,3},{3,2},{4,5},{5,4},{6,7},{7,6},{8,9},{9,8},{10,11... | collective-permute-start | bytes 24584 | tf_op jit(solution)/shard_map/ppermute | solution.py:359
  115.8 2.9 %ortho.1 = f32[1600,256]{1,0:T(8,128)} custom-call(f32[256,256]{1,0:T(8,128)S(1)} %inverse_factor.1.back.refs_4_, f32[1600,256]{1,0:T(8,128)S(1)} %pad_maximum_fusion.proj), custom_call_target="tpu_custom_call" | custom-call | flops 2305999872 | tf_op jit(solution)/shard_map/ortho/pallas_call | solution.py:265
  118.7 17.9 %new_weight.1.refs_2_ = f32[1600,2560]{1,0:T(8,128)} custom-call(f32[8,256]{1,0:T(8,128)S(1)} %add.80.squares, f32[1600,256]{1,0:T(8,128)} %ortho.1, f32[1600,2560]{1,0:T(8,128)} %weight.1, f32[256,1024]{1,0:T(8,128)S(1)} %get-tuple-element.51.refs_0_, f32[256,1536]{1,0:T(8,128)S(1)} %get-tuple-element.52.refs_1_), custom_call_target="tpu_custom_call" | custom-call | flops 11530000384 | tf_op jit(solution)/shard_map/new_weight/pallas_call | solution.py:346
  136.6 9.0 %new_momentum.1 = f32[1600,2560]{1,0:T(8,128)} custom-call(f32[1600,256]{1,0:T(8,128)} %ortho.1, bf16[1600,2560]{1,0:T(8,128)(2,1)S(1)} %bitcast.5, bf16[1600,2560]{1,0:T(8,128)(2,1)S(1)} %bitcast.7, f32[256,1024]{1,0:T(8,128)S(1)} %get-tuple-element.51.refs_0_, f32[256,1536]{1,0:T(8,128)S(1)} %get-tuple-element.52.refs_1_, f32[1600,2560]{1,0:T(8,128)} %new_weight.1.refs_2_), custom_call_target="tpu_custom_call" | custom-call | flops 11530000384 | tf_op jit(solution)/shard_map/new_momentum/pallas_call | solution.py:304
  (71 shorter events, 8.1 us)
Async XLA Ops:
  5.1 11.0 %collective-permute-start = (f32[256,256]{1,0:T(8,128)}, f32[256,256]{1,0:T(8,128)S(1)}, u32[]{:S(2)}, u32[]{:S(2)}) collective-permute-start(f32[256,256]{1,0:T(8,128)} %get-tuple-element.32.refs_0_), channel_id=1, source_target_pairs={{0,1},{1,0},{2,3},{3,2},{4,5},{5,4},{6,7},{7,6},{8,9},{9,8},{10,11... | collective-permute-start | bytes 786440 | tf_op jit(solution)/shard_map/ppermute | solution.py:359
  16.0 15.1 %collective-permute-start.1 = (f32[512,256]{1,0:T(8,128)}, f32[512,256]{1,0:T(8,128)S(1)}, u32[]{:S(2)}, u32[]{:S(2)}) collective-permute-start(f32[512,256]{1,0:T(8,128)} %get-tuple-element.35.refs_1_), channel_id=1, source_target_pairs={{0,1},{1,0},{2,3},{3,2},{4,5},{5,4},{6,7},{7,6},{8,9},{9,8},{10,11... | collective-permute-start | bytes 1572872 | tf_op jit(solution)/shard_map/ppermute | solution.py:359
  25.2 19.5 %collective-permute-start.3 = (f32[576,256]{1,0:T(8,128)}, f32[576,256]{1,0:T(8,128)S(1)}, u32[]{:S(2)}, u32[]{:S(2)}) collective-permute-start(f32[576,256]{1,0:T(8,128)} %get-tuple-element.39.refs_0_), channel_id=1, source_target_pairs={{0,1},{1,0},{2,3},{3,2},{4,5},{5,4},{6,7},{7,6},{8,9},{9,8},{10,11... | collective-permute-start | bytes 1769480 | tf_op jit(solution)/shard_map/ppermute | solution.py:359
  31.1 4.7 %copy-start.6 = (f32[512,256]{1,0:T(8,128)S(1)}, f32[512,256]{1,0:T(8,128)}, u32[]{:S(2)}) copy-start(f32[512,256]{1,0:T(8,128)} %get-tuple-element.35.refs_1_) | copy-start | bytes 1572868
  31.1 4.7 %copy-start.7 = (f32[256,256]{1,0:T(8,128)S(1)}, f32[256,256]{1,0:T(8,128)}, u32[]{:S(2)}) copy-start(f32[256,256]{1,0:T(8,128)} %get-tuple-element.32.refs_0_) | copy-start | bytes 786436
  35.7 16.6 %collective-permute-start.2 = (f32[256,256]{1,0:T(8,128)}, f32[256,256]{1,0:T(8,128)S(1)}, u32[]{:S(2)}, u32[]{:S(2)}) collective-permute-start(f32[256,256]{1,0:T(8,128)} %get-tuple-element.38.before.refs_0_), channel_id=1, source_target_pairs={{0,1},{1,0},{2,3},{3,2},{4,5},{5,4},{6,7},{7,6},{8,9},{9,8},{10,11... | collective-permute-start | bytes 786440 | tf_op jit(solution)/shard_map/ppermute | solution.py:359
  36.8 7.9 %copy-start.5 = (f32[576,256]{1,0:T(8,128)S(1)}, f32[576,256]{1,0:T(8,128)}, u32[]{:S(2)}) copy-start(f32[576,256]{1,0:T(8,128)} %get-tuple-element.39.refs_0_) | copy-start | bytes 1769476
  57.7 2.2 %collective-permute-start.4 = (f32[128,1280]{1,0:T(8,128)S(1)}, f32[128,1280]{1,0:T(8,128)S(1)}, u32[]{:S(2)}, u32[]{:S(2)}) collective-permute-start(f32[128,1280]{1,0:T(8,128)S(1)} %slice.40), channel_id=1, source_target_pairs={{0,2},{2,0},{4,6},{6,4},{8,10},{10,8},{12,14},{14,12},{16,18},{18,... | collective-permute-start | bytes 1966088 | tf_op jit(solution)/shard_map/ppermute | solution.py:359
  57.9 5.7 %collective-permute-start.9 = (f32[128,1536]{1,0:T(8,128)S(1)}, f32[128,1536]{1,0:T(8,128)S(1)}, u32[]{:S(2)}, u32[]{:S(2)}) collective-permute-start(f32[128,1536]{1,0:T(8,128)S(1)} %slice.46), channel_id=1, source_target_pairs={{0,2},{2,0},{4,6},{6,4},{8,10},{10,8},{12,14},{14,12},{16,18},{18,... | collective-permute-start | bytes 2359304 | tf_op jit(solution)/shard_map/ppermute | solution.py:359
  60.0 7.1 %collective-permute-start.7 = (f32[32,1280]{1,0:T(8,128)S(1)}, f32[32,1280]{1,0:T(8,128)S(1)}, u32[]{:S(2)}, u32[]{:S(2)}) collective-permute-start(f32[32,1280]{1,0:T(8,128)S(1)} %get-tuple-element.60), channel_id=1, source_target_pairs={{0,8},{2,10},{4,12},{6,14},{8,0},{10,2},{12,4},{14,6},{16,24},{18,... | collective-permute-start | bytes 491528 | tf_op jit(solution)/shard_map/ppermute | solution.py:359
  61.7 10.0 %collective-permute-start.6 = (f32[32,1280]{1,0:T(8,128)S(1)}, f32[32,1280]{1,0:T(8,128)S(1)}, u32[]{:S(2)}, u32[]{:S(2)}) collective-permute-start(f32[32,1280]{1,0:T(8,128)S(1)} %get-tuple-element.61), channel_id=1, source_target_pairs={{0,12},{2,14},{4,8},{6,10},{8,4},{10,6},{12,0},{14,2},{16,28},{18,... | collective-permute-start | bytes 491528 | tf_op jit(solution)/shard_map/ppermute | solution.py:359
  63.1 10.5 %collective-permute-start.5 = (f32[32,1280]{1,0:T(8,128)S(1)}, f32[32,1280]{1,0:T(8,128)S(1)}, u32[]{:S(2)}, u32[]{:S(2)}) collective-permute-start(f32[32,1280]{1,0:T(8,128)S(1)} %get-tuple-element.59), channel_id=1, source_target_pairs={{0,4},{2,6},{4,0},{6,2},{8,12},{10,14},{12,8},{14,10},{16,20},{18,... | collective-permute-start | bytes 491528 | tf_op jit(solution)/shard_map/ppermute | solution.py:359
  63.8 12.9 %collective-permute-start.12 = (f32[32,1536]{1,0:T(8,128)S(1)}, f32[32,1536]{1,0:T(8,128)S(1)}, u32[]{:S(2)}, u32[]{:S(2)}) collective-permute-start(f32[32,1536]{1,0:T(8,128)S(1)} %get-tuple-element.57), channel_id=1, source_target_pairs={{0,8},{2,10},{4,12},{6,14},{8,0},{10,2},{12,4},{14,6},{16,24},{18,... | collective-permute-start | bytes 589832 | tf_op jit(solution)/shard_map/ppermute | solution.py:359
  65.4 17.4 %collective-permute-start.11 = (f32[32,1536]{1,0:T(8,128)S(1)}, f32[32,1536]{1,0:T(8,128)S(1)}, u32[]{:S(2)}, u32[]{:S(2)}) collective-permute-start(f32[32,1536]{1,0:T(8,128)S(1)} %get-tuple-element.58), channel_id=1, source_target_pairs={{0,12},{2,14},{4,8},{6,10},{8,4},{10,6},{12,0},{14,2},{16,28},{18,... | collective-permute-start | bytes 589832 | tf_op jit(solution)/shard_map/ppermute | solution.py:359
  67.1 15.7 %collective-permute-start.10 = (f32[32,1536]{1,0:T(8,128)S(1)}, f32[32,1536]{1,0:T(8,128)S(1)}, u32[]{:S(2)}, u32[]{:S(2)}) collective-permute-start(f32[32,1536]{1,0:T(8,128)S(1)} %get-tuple-element.56), channel_id=1, source_target_pairs={{0,4},{2,6},{4,0},{6,2},{8,12},{10,14},{12,8},{14,10},{16,20},{18,... | collective-permute-start | bytes 589832 | tf_op jit(solution)/shard_map/ppermute | solution.py:359
  73.6 9.8 %collective-permute-start.8 = (f32[32,1280]{1,0:T(8,128)S(1)}, f32[32,1280]{1,0:T(8,128)S(1)}, u32[]{:S(2)}, u32[]{:S(2)}) collective-permute-start(f32[32,1280]{1,0:T(8,128)S(1)} %fusion.6.x), channel_id=1, source_target_pairs={{0,16},{2,18},{4,20},{6,22},{8,24},{10,26},{12,28},{14,30},{16,0},... | collective-permute-start | bytes 491528 | tf_op jit(solution)/shard_map/ppermute | solution.py:359
  82.9 11.4 %collective-permute-start.16 = (f32[32,1536]{1,0:T(8,128)S(1)}, f32[32,1536]{1,0:T(8,128)S(1)}, u32[]{:S(2)}, u32[]{:S(2)}) collective-permute-start(f32[32,1536]{1,0:T(8,128)S(1)} %fusion.4.before), channel_id=1, source_target_pairs={{0,16},{2,18},{4,20},{6,22},{8,24},{10,26},{12,28},{14,30},{16,0},... | collective-permute-start | bytes 589832 | tf_op jit(solution)/shard_map/ppermute | solution.py:359
  83.4 11.2 %collective-permute-start.13 = (f32[32,1280]{1,0:T(8,128)S(1)}, f32[32,1280]{1,0:T(8,128)S(1)}, u32[]{:S(2)}, u32[]{:S(2)}) collective-permute-start(f32[32,1280]{1,0:T(8,128)S(1)} %add_pieces.1.refs_0_), channel_id=1, source_target_pairs={{0,8},{2,10},{4,12},{6,14},{8,0},{10,2},{12,4},{14,6},{16,24},{18,... | collective-permute-start | bytes 491528 | tf_op jit(solution)/shard_map/ppermute | solution.py:359
  86.5 8.1 %collective-permute-start.14 = (f32[32,1280]{1,0:T(8,128)S(1)}, f32[32,1280]{1,0:T(8,128)S(1)}, u32[]{:S(2)}, u32[]{:S(2)}) collective-permute-start(f32[32,1280]{1,0:T(8,128)S(1)} %add_pieces.1.refs_0_), channel_id=1, source_target_pairs={{0,4},{2,6},{4,0},{6,2},{8,12},{10,14},{12,8},{14,10},{16,20},{18,... | collective-permute-start | bytes 491528 | tf_op jit(solution)/shard_map/ppermute | solution.py:359
  86.5 10.5 %collective-permute-start.15 = (f32[32,1280]{1,0:T(8,128)S(1)}, f32[32,1280]{1,0:T(8,128)S(1)}, u32[]{:S(2)}, u32[]{:S(2)}) collective-permute-start(f32[32,1280]{1,0:T(8,128)S(1)} %add_pieces.1.refs_0_), channel_id=1, source_target_pairs={{0,12},{2,14},{4,8},{6,10},{8,4},{10,6},{12,0},{14,2},{16,28},{18,... | collective-permute-start | bytes 491528 | tf_op jit(solution)/shard_map/ppermute | solution.py:359
  97.0 13.2 %copy-start.1 = (f32[128,1280]{1,0:T(8,128)}, f32[128,1280]{1,0:T(8,128)S(1)}, u32[]{:S(2)}) copy-start(f32[128,1280]{1,0:T(8,128)S(1)} %join_pieces.2.own) | copy-start | bytes 1966084
  97.1 3.6 %collective-permute-start.17 = (f32[128,1280]{1,0:T(8,128)S(1)}, f32[128,1280]{1,0:T(8,128)S(1)}, u32[]{:S(2)}, u32[]{:S(2)}) collective-permute-start(f32[128,1280]{1,0:T(8,128)S(1)} %join_pieces.2.own), channel_id=1, source_target_pairs={{0,2},{2,0},{4,6},{6,4},{8,10},{10,8},{12,14},{14,12},{16,18},{18,... | collective-permute-start | bytes 1966088 | tf_op jit(solution)/shard_map/ppermute | solution.py:359
  97.1 13.1 %collective-permute-start.18 = (f32[32,1536]{1,0:T(8,128)S(1)}, f32[32,1536]{1,0:T(8,128)S(1)}, u32[]{:S(2)}, u32[]{:S(2)}) collective-permute-start(f32[32,1536]{1,0:T(8,128)S(1)} %add.78.refs_4_.before.refs_0_), channel_id=1, source_target_pairs={{0,8},{2,10},{4,12},{6,14},{8,0},{10,2},{12,4},{14,6},{16,24},{18,... | collective-permute-start | bytes 589832 | tf_op jit(solution)/shard_map/ppermute | solution.py:359
  97.3 12.9 %collective-permute-start.19 = (f32[32,1536]{1,0:T(8,128)S(1)}, f32[32,1536]{1,0:T(8,128)S(1)}, u32[]{:S(2)}, u32[]{:S(2)}) collective-permute-start(f32[32,1536]{1,0:T(8,128)S(1)} %add.78.refs_4_.before.refs_0_), channel_id=1, source_target_pairs={{0,4},{2,6},{4,0},{6,2},{8,12},{10,14},{12,8},{14,10},{16,20},{18,... | collective-permute-start | bytes 589832 | tf_op jit(solution)/shard_map/ppermute | solution.py:359
  99.0 11.3 %collective-permute-start.20 = (f32[32,1536]{1,0:T(8,128)S(1)}, f32[32,1536]{1,0:T(8,128)S(1)}, u32[]{:S(2)}, u32[]{:S(2)}) collective-permute-start(f32[32,1536]{1,0:T(8,128)S(1)} %add.78.refs_4_.before.refs_0_), channel_id=1, source_target_pairs={{0,12},{2,14},{4,8},{6,10},{8,4},{10,6},{12,0},{14,2},{16,28},{18,... | collective-permute-start | bytes 589832 | tf_op jit(solution)/shard_map/ppermute | solution.py:359
  100.7 9.6 %copy-start.3 = (f32[128,1280]{1,0:T(8,128)}, f32[128,1280]{1,0:T(8,128)S(1)}, u32[]{:S(2)}) copy-start(f32[128,1280]{1,0:T(8,128)S(1)} %collective-permute-done.17.other) | copy-start | bytes 1966084
  110.3 2.4 %collective-permute-start.21 = (f32[128,1536]{1,0:T(8,128)S(1)}, f32[128,1536]{1,0:T(8,128)S(1)}, u32[]{:S(2)}, u32[]{:S(2)}) collective-permute-start(f32[128,1536]{1,0:T(8,128)S(1)} %join_pieces.3.own), channel_id=1, source_target_pairs={{0,2},{2,0},{4,6},{6,4},{8,10},{10,8},{12,14},{14,12},{16,18},{18,... | collective-permute-start | bytes 2359304 | tf_op jit(solution)/shard_map/ppermute | solution.py:359
  113.7 5.0 %collective-permute-start.22 = (f32[8,256]{1,0:T(8,128)S(1)}, f32[8,256]{1,0:T(8,128)S(1)}, u32[]{:S(2)}, u32[]{:S(2)}) collective-permute-start(f32[8,256]{1,0:T(8,128)S(1)} %add.79), channel_id=1, source_target_pairs={{0,1},{1,0},{2,3},{3,2},{4,5},{5,4},{6,7},{7,6},{8,9},{9,8},{10,11... | collective-permute-start | bytes 24584 | tf_op jit(solution)/shard_map/ppermute | solution.py:359
  115.8 20.8 %slice-start = ((s8[8192000]{0:T(1024)(128)(4,1)}), s8[4194304]{0:T(1024)(128)(4,1)S(1)}, s32[]{:S(2)}) async-start(s8[8192000]{0:T(1024)(128)(4,1)} %bitcast.4), calls=%async_computation | async-start | bytes 8388608
  115.8 20.8 %slice-start.2 = ((s8[8192000]{0:T(1024)(128)(4,1)}), s8[4194304]{0:T(1024)(128)(4,1)S(1)}, s32[]{:S(2)}) async-start(s8[8192000]{0:T(1024)(128)(4,1)} %bitcast.6), calls=%async_computation.2 | async-start | bytes 8388608
  118.7 17.9 %slice-start.1 = ((s8[8192000]{0:T(1024)(128)(4,1)}), s8[3997696]{0:T(1024)(128)(4,1)S(1)}, s32[]{:S(2)}) async-start(s8[8192000]{0:T(1024)(128)(4,1)} %bitcast.4), calls=%async_computation.1 | async-start | bytes 7995392
  118.7 17.9 %slice-start.3 = ((s8[8192000]{0:T(1024)(128)(4,1)}), s8[3997696]{0:T(1024)(128)(4,1)S(1)}, s32[]{:S(2)}) async-start(s8[8192000]{0:T(1024)(128)(4,1)} %bitcast.6), calls=%async_computation.3 | async-start | bytes 7995392
  (3 other events, 3.3 us)
